TPU v7x, 256 devices: a whole 4x4x8 slice. The times are simulated.
256 devices in a mesh: box: 64 (over x, z, y_hi), rhs: 4 (over y_lo, core).
Axes of the slice: x: 4, y: 4 (y_hi: 2, y_lo: 2; y = y_hi * 2 + y_lo), z: 8, core: 2. Of those that a mesh axis runs over, the one named last changes fastest.
Arguments:
- rhs_block: float32 [256, 256, 512], P('box', 'rhs'), may hold values from -6 to 6
- near_blocks: float32 [256, 3, 256, 512], P('box'), may hold values from -0.15625 to 0.15625
- near_mask: int32 [2, 256], P(None, 'box'), may hold values 0 or 1
- compress: float32 [256, 256, 128], P('box'), may hold values from -0.25 to 0.25
- butterfly: float32 [8, 256, 2, 64, 128], P(None, 'box'), may hold values from -0.375 to 0.375
- expand: float32 [256, 64, 512], P('box'), may hold values from -0.5 to 0.5
Outputs:
- field: float32 [256, 256, 512], P('box', 'rhs')
All inputs are finite; a program needn't handle non-finite values. No bound on the sum of `near_mask` on one device may be relied on, other than what follows from the above.
Results may differ from a plain program's by a relative error of at most 0.0001.
Values sent between devices are 32-bit elements; how exact they have to be, the bound alone decides.
No kernel may reach another device: no remote copies, remote signals or barrier semaphores. Data moves between devices by JAX's collectives and lax.ppermute only.
A program may use at most 64 MiB of HBM per device.

v0:
```python
import jax
import jax.numpy as jnp
from jax import lax
from jax.sharding import PartitionSpec as P


def padded(block, sides, width):
    for axis, dim in sides:
        count = lax.axis_size(axis)
        forward = [(i, i + 1) for i in range(count - 1)]
        forward.append((count - 1, 0))
        backward = [(target, source) for source, target in forward]
        low = lax.ppermute(
            lax.slice_in_dim(block, block.shape[dim] - width, None, axis=dim), axis, forward
        )
        high = lax.ppermute(lax.slice_in_dim(block, 0, width, axis=dim), axis, backward)
        block = jnp.concatenate([low, block, high], axis=dim)
    return block


def partner(value, axis, apart):
    mask = 2**apart
    pairs = [(source, source ^ mask) for source in range(lax.axis_size(axis))]
    return lax.ppermute(value, axis, pairs)


def complex_apply(values, weights):
    half = values.shape[-1] // 2
    width = weights.shape[-1] // 2
    real_in = jnp.einsum(
        "bri,bio->bro", values[..., :half], weights, precision=lax.Precision.HIGHEST
    )
    imag_in = jnp.einsum(
        "bri,bio->bro", values[..., half:], weights, precision=lax.Precision.HIGHEST
    )
    real_out = real_in[..., :width] - imag_in[..., width:]
    imag_out = real_in[..., width:] + imag_in[..., :width]
    return jnp.concatenate([real_out, imag_out], axis=-1)


def local_partner(coef, level):
    half = 2**level
    shaped = coef.reshape(coef.shape[0] // (2 * half), 2, half, coef.shape[1], coef.shape[2])
    return jnp.flip(shaped, 1).reshape(coef.shape)


def near_field(rhs_block, near_blocks, near_mask, count):
    extended = padded(rhs_block, (("box", 0),), 1)
    masks = near_mask.astype(jnp.float32)
    before = complex_apply(extended[0:count], near_blocks[:, 0])
    middle = complex_apply(rhs_block, near_blocks[:, 1])
    after = complex_apply(extended[2 : count + 2], near_blocks[:, 2])
    return before * masks[0][:, None, None] + middle + after * masks[1][:, None, None]


def far_field(rhs_block, compress, butterfly, expand, count):
    coef = complex_apply(rhs_block, compress)
    local_bits = count.bit_length() - 1
    for level in range(butterfly.shape[0]):
        weights = butterfly[level]
        if level < local_bits:
            other = local_partner(coef, level)
        else:
            other = partner(coef, "box", level - local_bits)
        coef = complex_apply(coef, weights[:, 0]) + complex_apply(other, weights[:, 1])
    return complex_apply(coef, expand)


def on_device(rhs_block, near_blocks, near_mask, compress, butterfly, expand):
    count = rhs_block.shape[0]
    near = near_field(rhs_block, near_blocks, near_mask, count)
    far = far_field(rhs_block, compress, butterfly, expand, count)
    return near + far


def solution(mesh):
    placed = (
        P("box", "rhs", None),
        P("box", None, None, None),
        P(None, "box"),
        P("box", None, None),
        P(None, "box", None, None, None),
        P("box", None, None),
    )
    return jax.shard_map(
        on_device, mesh=mesh, in_specs=placed, out_specs=P("box", "rhs", None), check_vma=False
    )
```

profile of v0, /device:TPU:8, one launch (start us, length us, event | category | flops | bytes accessed | tf_op | source)
XLA Modules:
  0.0 74.0 jit_solution(1968167406355501525)
XLA Ops:
  0.0 1.6 %fusion.25 = f32[4,64,128]{2,1,0:T(8,128)S(1)} fusion(f32[4,256,128]{2,1,0:T(8,128)} %param.9, f32[4,64,512]{2,1,0:T(8,128)} %param.6), kind=kOutput, calls=%fused_computation.43 | convolution fusion | flops 100663296 | bytes 917504 | tf_op jit(solution)/shard_map/bri,bio->bro/dot_general | solution.py:33
  1.6 1.6 %fusion.28 = f32[4,64,128]{2,1,0:T(8,128)S(1)} fusion(f32[4,256,128]{2,1,0:T(8,128)} %param.9, f32[4,64,512]{2,1,0:T(8,128)} %param.6), kind=kOutput, calls=%fused_computation.46 | convolution fusion | flops 100663296 | bytes 917504 | tf_op jit(solution)/shard_map/bri,bio->bro/dot_general | solution.py:30
  3.2 2.8 %fusion.97 = (f32[1,4,2,64,128]{4,3,2,1,0:T(8,128)}, f32[1,4,2,64,128]{4,3,2,1,0:T(8,128)}, f32[1,4,2,64,128]{4,3,2,1,0:T(8,128)}, f32[1,4,2,64,128]{4,3,2,1,0:T...) fusion(f32[8,4,2,64,128]{4,3,2,1,0:T(8,128)} %param.10), kind=kLoop, calls=%fused_computation.181 | loop fusion | bytes 4194304 | tf_op jit(solution)/shard_map/slice | solution.py:60
  6.3 1.1 %copy_bitcast_fusion.6 = (f32[4,2,64,128]{3,2,0,1:T(8,128)S(1)}, f32[4,2,64,128]{3,2,0,1:T(8,128)S(1)}) fusion(f32[1,4,2,64,128]{4,3,2,1,0:T(8,128)S(1)} %get-tuple-element.11, f32[1,4,2,64,128]{4,3,2,1,0:T(8,128)} %get-tuple-element.12), kind=kLoop, calls=%fused_computation.41 | loop fusion | bytes 1048576 | tf_op jit(solution)/shard_map/squeeze | solution.py:60
  7.4 0.3 fusion.91
  8.8 0.8 %maximum_add_fusion.2 = f32[1,2,2,64,128]{4,3,2,1,0:T(8,128)} fusion(f32[1,2,2,64,64]{4,3,2,1,0:T(8,128)S(1)} %bitcast.157, f32[1,2,2,64,64]{4,3,2,1,0:T(8,128)S(1)} %bitcast.156, f32[1,2,2,64,64]{4,3,2,1,0:T(8,128)S(1)} %bitcast.155, f32[1,2,2,64,64]{4,3,2,1,0:T(8,128)S(1)} %bitcast.154), kind=kLoop, calls=%fused_computation.166 | loop fusion | flops 98304 | bytes 393216 | tf_op jit(solution)/shard_map/add | solution.py:65
  9.6 0.9 %rev.9 = f32[1,2,2,64,128]{4,3,2,1,0:T(8,128)S(1)} reverse(f32[1,2,2,64,128]{4,3,2,1,0:T(8,128)} %maximum_add_fusion.2), dimensions={1} | reverse | bytes 262144 | tf_op jit(solution)/shard_map/jit(_flip)/rev | solution.py:44
  10.8 0.3 fusion.83
  12.3 2.4 %collective-permute-start.2 = (f32[4,64,128]{2,1,0:T(8,128)S(1)}, f32[4,64,128]{2,1,0:T(8,128)S(1)}, u32[]{:S(2)}, u32[]{:S(2)}) collective-permute-start(f32[4,64,128]{2,1,0:T(8,128)S(1)} %maximum_add_fusion.1), channel_id=1, source_target_pairs={{0,4},{4,0},{8,12},{12,8},{16,20},{20,16},{24,28},{28,24},{32,36},... | collective-permute-start | bytes 393224 | tf_op jit(solution)/shard_map/ppermute | solution.py:24
  14.7 1.3 %collective-permute-start = (f32[1,64,512]{2,1,0:T(8,128)S(1)}, f32[1,64,512]{2,1,0:T(8,128)S(1)}, u32[]{:S(2)}, u32[]{:S(2)}) collective-permute-start(f32[1,64,512]{2,1,0:T(8,128)S(1)} %get-tuple-element.22), channel_id=1, source_target_pairs={{0,4},{4,8},{8,12},{12,16},{16,20},{20,24},{24,28},{28,32},{32,36}... | collective-permute-start | bytes 393224 | tf_op jit(solution)/shard_map/ppermute | solution.py:13
  16.0 7.6 %collective-permute-start.1 = (f32[1,64,512]{2,1,0:T(8,128)S(1)}, f32[1,64,512]{2,1,0:T(8,128)S(1)}, u32[]{:S(2)}, u32[]{:S(2)}) collective-permute-start(f32[1,64,512]{2,1,0:T(8,128)S(1)} %get-tuple-element.21), channel_id=1, source_target_pairs={{4,0},{8,4},{12,8},{16,12},{20,16},{24,20},{28,24},{32,28},{36,32}... | collective-permute-start | bytes 393224 | tf_op jit(solution)/shard_map/ppermute | solution.py:16
  23.8 0.3 fusion.79
  24.2 3.0 %fusion.4 = f32[4,64,512]{2,1,0:T(8,128)S(1)} fusion(f32[4,3,256,512]{3,2,1,0:T(8,128)} %param.7, f32[4,64,512]{2,1,0:T(8,128)S(1)} %copy-done.1), kind=kOutput, calls=%fused_computation.4 | convolution fusion | flops 402653184 | bytes 2883584 | tf_op jit(solution)/shard_map/bri,bio->bro/dot_general | solution.py:33
  27.2 1.4 %fusion.6 = f32[4,64,512]{2,1,0:T(8,128)S(1)} fusion(f32[4,3,256,512]{3,2,1,0:T(8,128)S(1)} %bitcast.125, f32[4,64,512]{2,1,0:T(8,128)S(1)} %copy-done.1), kind=kOutput, calls=%fused_computation.6 | convolution fusion | flops 402653184 | bytes 2883584 | tf_op jit(solution)/shard_map/bri,bio->bro/dot_general | solution.py:30
  29.3 0.3 fusion.75
  30.5 0.3 fusion.71
  31.0 1.4 %fusion = f32[4,64,512]{2,1,0:T(8,128)S(1)} fusion(f32[4,3,256,512]{3,2,1,0:T(8,128)S(1)} %bitcast.125, f32[5,64,512]{2,1,0:T(8,128)S(1)} %constant_dynamic-update-slice_fusion.2), kind=kOutput, calls=%fused_computation | convolution fusion | flops 402653184 | bytes 2883584 | tf_op jit(solution)/shard_map/bri,bio->bro/dot_general | solution.py:33
  32.4 1.4 %fusion.2 = f32[4,64,512]{2,1,0:T(8,128)S(1)} fusion(f32[4,3,256,512]{3,2,1,0:T(8,128)S(1)} %bitcast.125, f32[5,64,512]{2,1,0:T(8,128)S(1)} %constant_dynamic-update-slice_fusion.2), kind=kOutput, calls=%fused_computation.2 | convolution fusion | flops 402653184 | bytes 2883584 | tf_op jit(solution)/shard_map/bri,bio->bro/dot_general | solution.py:30
  33.8 1.4 %fusion.10 = f32[4,64,512]{2,1,0:T(8,128)S(1)} fusion(f32[4,3,256,512]{3,2,1,0:T(8,128)S(1)} %bitcast.125, f32[5,64,512]{2,1,0:T(8,128)S(1)} %get-tuple-element.24), kind=kOutput, calls=%fused_computation.10 | convolution fusion | flops 402653184 | bytes 2883584 | tf_op jit(solution)/shard_map/bri,bio->bro/dot_general | solution.py:30
  35.1 1.4 %fusion.8 = f32[4,64,512]{2,1,0:T(8,128)S(1)} fusion(f32[4,3,256,512]{3,2,1,0:T(8,128)S(1)} %bitcast.125, f32[5,64,512]{2,1,0:T(8,128)S(1)} %get-tuple-element.24), kind=kOutput, calls=%fused_computation.8 | convolution fusion | flops 402653184 | bytes 2883584 | tf_op jit(solution)/shard_map/bri,bio->bro/dot_general | solution.py:33
  37.1 0.3 fusion.67
  37.7 0.8 %collective-permute-start.4 = (f32[4,64,128]{2,1,0:T(8,128)S(1)}, f32[4,64,128]{2,1,0:T(8,128)S(1)}, u32[]{:S(2)}, u32[]{:S(2)}) collective-permute-start(f32[4,64,128]{2,1,0:T(8,128)S(1)} %maximum_add_fusion.4), channel_id=1, source_target_pairs={{0,16},{4,20},{8,24},{12,28},{16,0},{20,4},{24,8},{28,12},{32,48},... | collective-permute-start | bytes 393224 | tf_op jit(solution)/shard_map/ppermute | solution.py:24
  38.8 0.3 fusion.63
  39.3 6.9 %collective-permute-done.4 = f32[4,64,128]{2,1,0:T(8,128)S(1)} collective-permute-done((f32[4,64,128]{2,1,0:T(8,128)S(1)}, f32[4,64,128]{2,1,0:T(8,128)S(1)}, u32[]{:S(2)}, u32[]{:S(2)}) %collective-permute-start.4) | collective-permute-done | bytes 131104 | tf_op jit(solution)/shard_map/ppermute | solution.py:24
  47.0 3.8 %collective-permute-start.5 = (f32[4,64,128]{2,1,0:T(8,128)S(1)}, f32[4,64,128]{2,1,0:T(8,128)S(1)}, u32[]{:S(2)}, u32[]{:S(2)}) collective-permute-start(f32[4,64,128]{2,1,0:T(8,128)S(1)} %maximum_add_fusion.5), channel_id=1, source_target_pairs={{0,32},{4,36},{8,40},{12,44},{16,48},{20,52},{24,56},{28,60},{32,0... | collective-permute-start | bytes 393224 | tf_op jit(solution)/shard_map/ppermute | solution.py:24
  51.6 5.8 %collective-permute-done.5 = f32[4,64,128]{2,1,0:T(8,128)S(1)} collective-permute-done((f32[4,64,128]{2,1,0:T(8,128)S(1)}, f32[4,64,128]{2,1,0:T(8,128)S(1)}, u32[]{:S(2)}, u32[]{:S(2)}) %collective-permute-start.5) | collective-permute-done | bytes 131104 | tf_op jit(solution)/shard_map/ppermute | solution.py:24
  57.7 0.3 fusion.51
  59.1 4.3 %collective-permute-done.6 = f32[4,64,128]{2,1,0:T(8,128)S(1)} collective-permute-done((f32[4,64,128]{2,1,0:T(8,128)S(1)}, f32[4,64,128]{2,1,0:T(8,128)S(1)}, u32[]{:S(2)}, u32[]{:S(2)}) %collective-permute-start.6) | collective-permute-done | bytes 131104 | tf_op jit(solution)/shard_map/ppermute | solution.py:24
  65.1 5.7 %collective-permute-done.7 = f32[4,64,128]{2,1,0:T(8,128)S(1)} collective-permute-done((f32[4,64,128]{2,1,0:T(8,128)S(1)}, f32[4,64,128]{2,1,0:T(8,128)S(1)}, u32[]{:S(2)}, u32[]{:S(2)}) %collective-permute-start.7) | collective-permute-done | bytes 131104 | tf_op jit(solution)/shard_map/ppermute | solution.py:24
  71.8 0.6 fusion.31
  72.4 0.6 fusion.33
  73.0 1.0 %fusion.20 = f32[4,64,512]{2,1,0:T(8,128)} fusion(f32[4,64,256]{2,1,0:T(8,128)S(1)} %get-tuple-element.63, f32[4,64,256]{2,1,0:T(8,128)S(1)} %get-tuple-element.64, f32[4,64,256]{2,1,0:T(8,128)S(1)} %get-tuple-element.18, f32[4,64,256]{2,1,0:T(8,128)S(1)} %get-tuple-element.17, f32[4,64,256]{2,1,0:T(8,128)S(1)} %get-tuple-element.16, ...), kind=kLoop, calls=%fused_computation.21 | loop fusion | flops 1179648 | bytes 2621472 | tf_op jit(solution)/shard_map/add | solution.py:73
  (96 shorter events, 11.1 us)
Async XLA Ops:
  0.0 71.8 %copy-start = (f32[4,64,512]{2,1,0:T(8,128)S(1)}, f32[4,64,512]{2,1,0:T(8,128)}, u32[]{:S(2)}) copy-start(f32[4,64,512]{2,1,0:T(8,128)} %param.11) | copy-start | bytes 1572868
  6.1 21.0 %slice-start = ((s8[6291456]{0:T(1024)(128)(4,1)}), s8[2097152]{0:T(1024)(128)(4,1)S(1)}, s32[]{:S(2)}) async-start(s8[6291456]{0:T(1024)(128)(4,1)} %bitcast.124), calls=%async_computation | async-start | bytes 4194304
  10.7 3.9 %copy-start.1 = (f32[4,64,512]{2,1,0:T(8,128)S(1)}, f32[4,64,512]{2,1,0:T(8,128)}, u32[]{:S(2)}) copy-start(f32[4,64,512]{2,1,0:T(8,128)} %param.6) | copy-start | bytes 1572868
  11.1 12.5 %copy-start.7 = (f32[1,4,2,64,128]{4,3,2,1,0:T(8,128)S(1)}, f32[1,4,2,64,128]{4,3,2,1,0:T(8,128)}, u32[]{:S(2)}) copy-start(f32[1,4,2,64,128]{4,3,2,1,0:T(8,128)} %get-tuple-element.10) | copy-start | bytes 786436
  11.2 15.9 %slice-start.1 = ((s8[6291456]{0:T(1024)(128)(4,1)}), s8[4194304]{0:T(1024)(128)(4,1)S(1)}, s32[]{:S(2)}) async-start(s8[6291456]{0:T(1024)(128)(4,1)} %bitcast.124), calls=%async_computation.1 | async-start | bytes 8388608
  12.3 16.8 %collective-permute-start.2 = (f32[4,64,128]{2,1,0:T(8,128)S(1)}, f32[4,64,128]{2,1,0:T(8,128)S(1)}, u32[]{:S(2)}, u32[]{:S(2)}) collective-permute-start(f32[4,64,128]{2,1,0:T(8,128)S(1)} %maximum_add_fusion.1), channel_id=1, source_target_pairs={{0,4},{4,0},{8,12},{12,8},{16,20},{20,16},{24,28},{28,24},{32,36},... | collective-permute-start | bytes 393224 | tf_op jit(solution)/shard_map/ppermute | solution.py:24
  14.7 16.1 %collective-permute-start = (f32[1,64,512]{2,1,0:T(8,128)S(1)}, f32[1,64,512]{2,1,0:T(8,128)S(1)}, u32[]{:S(2)}, u32[]{:S(2)}) collective-permute-start(f32[1,64,512]{2,1,0:T(8,128)S(1)} %get-tuple-element.22), channel_id=1, source_target_pairs={{0,4},{4,8},{8,12},{12,16},{16,20},{20,24},{24,28},{28,32},{32,36}... | collective-permute-start | bytes 393224 | tf_op jit(solution)/shard_map/ppermute | solution.py:13
  16.0 15.0 %collective-permute-start.1 = (f32[1,64,512]{2,1,0:T(8,128)S(1)}, f32[1,64,512]{2,1,0:T(8,128)S(1)}, u32[]{:S(2)}, u32[]{:S(2)}) collective-permute-start(f32[1,64,512]{2,1,0:T(8,128)S(1)} %get-tuple-element.21), channel_id=1, source_target_pairs={{4,0},{8,4},{12,8},{16,12},{20,16},{24,20},{28,24},{32,28},{36,32}... | collective-permute-start | bytes 393224 | tf_op jit(solution)/shard_map/ppermute | solution.py:16
  27.2 1.4 %copy-start.6 = (f32[1,4,2,64,128]{4,3,2,1,0:T(8,128)S(1)}, f32[1,4,2,64,128]{4,3,2,1,0:T(8,128)}, u32[]{:S(2)}) copy-start(f32[1,4,2,64,128]{4,3,2,1,0:T(8,128)} %get-tuple-element.9) | copy-start | bytes 786436
  27.2 1.5 %copy-start.5 = (f32[1,4,2,64,128]{4,3,2,1,0:T(8,128)S(1)}, f32[1,4,2,64,128]{4,3,2,1,0:T(8,128)}, u32[]{:S(2)}) copy-start(f32[1,4,2,64,128]{4,3,2,1,0:T(8,128)} %get-tuple-element.8) | copy-start | bytes 786436
  27.2 1.5 %copy-start.4 = (f32[1,4,2,64,128]{4,3,2,1,0:T(8,128)S(1)}, f32[1,4,2,64,128]{4,3,2,1,0:T(8,128)}, u32[]{:S(2)}) copy-start(f32[1,4,2,64,128]{4,3,2,1,0:T(8,128)} %get-tuple-element.7) | copy-start | bytes 786436
  27.2 1.5 %copy-start.3 = (f32[1,4,2,64,128]{4,3,2,1,0:T(8,128)S(1)}, f32[1,4,2,64,128]{4,3,2,1,0:T(8,128)}, u32[]{:S(2)}) copy-start(f32[1,4,2,64,128]{4,3,2,1,0:T(8,128)} %get-tuple-element.6) | copy-start | bytes 786436
  27.2 1.6 %copy-start.2 = (f32[1,4,2,64,128]{4,3,2,1,0:T(8,128)S(1)}, f32[1,4,2,64,128]{4,3,2,1,0:T(8,128)}, u32[]{:S(2)}) copy-start(f32[1,4,2,64,128]{4,3,2,1,0:T(8,128)} %get-tuple-element.5) | copy-start | bytes 786436
  27.2 1.6 %copy-start.8 = (s32[2,4]{1,0:T(2,128)S(1)}, s32[2,4]{1,0:T(2,128)}, u32[]{:S(2)}) copy-start(s32[2,4]{1,0:T(2,128)} %param.8) | copy-start | bytes 100
  29.9 6.9 %collective-permute-start.3 = (f32[4,64,128]{2,1,0:T(8,128)S(1)}, f32[4,64,128]{2,1,0:T(8,128)S(1)}, u32[]{:S(2)}, u32[]{:S(2)}) collective-permute-start(f32[4,64,128]{2,1,0:T(8,128)S(1)} %maximum_add_fusion.3), channel_id=1, source_target_pairs={{0,8},{4,12},{8,0},{12,4},{16,24},{20,28},{24,16},{28,20},{32,40},... | collective-permute-start | bytes 393224 | tf_op jit(solution)/shard_map/ppermute | solution.py:24
  37.7 8.5 %collective-permute-start.4 = (f32[4,64,128]{2,1,0:T(8,128)S(1)}, f32[4,64,128]{2,1,0:T(8,128)S(1)}, u32[]{:S(2)}, u32[]{:S(2)}) collective-permute-start(f32[4,64,128]{2,1,0:T(8,128)S(1)} %maximum_add_fusion.4), channel_id=1, source_target_pairs={{0,16},{4,20},{8,24},{12,28},{16,0},{20,4},{24,8},{28,12},{32,48},... | collective-permute-start | bytes 393224 | tf_op jit(solution)/shard_map/ppermute | solution.py:24
  47.0 10.4 %collective-permute-start.5 = (f32[4,64,128]{2,1,0:T(8,128)S(1)}, f32[4,64,128]{2,1,0:T(8,128)S(1)}, u32[]{:S(2)}, u32[]{:S(2)}) collective-permute-start(f32[4,64,128]{2,1,0:T(8,128)S(1)} %maximum_add_fusion.5), channel_id=1, source_target_pairs={{0,32},{4,36},{8,40},{12,44},{16,48},{20,52},{24,56},{28,60},{32,0... | collective-permute-start | bytes 393224 | tf_op jit(solution)/shard_map/ppermute | solution.py:24
  58.3 5.2 %collective-permute-start.6 = (f32[4,64,128]{2,1,0:T(8,128)S(1)}, f32[4,64,128]{2,1,0:T(8,128)S(1)}, u32[]{:S(2)}, u32[]{:S(2)}) collective-permute-start(f32[4,64,128]{2,1,0:T(8,128)S(1)} %maximum_add_fusion.6), channel_id=1, source_target_pairs={{0,64},{4,68},{8,72},{12,76},{16,80},{20,84},{24,88},{28,92},{32,9... | collective-permute-start | bytes 393224 | tf_op jit(solution)/shard_map/ppermute | solution.py:24
  64.3 6.6 %collective-permute-start.7 = (f32[4,64,128]{2,1,0:T(8,128)S(1)}, f32[4,64,128]{2,1,0:T(8,128)S(1)}, u32[]{:S(2)}, u32[]{:S(2)}) collective-permute-start(f32[4,64,128]{2,1,0:T(8,128)S(1)} %maximum_add_fusion.7), channel_id=1, source_target_pairs={{0,128},{4,132},{8,136},{12,140},{16,144},{20,148},{24,152},{28,15... | collective-permute-start | bytes 393224 | tf_op jit(solution)/shard_map/ppermute | solution.py:24
where the time goes:
time: 74.3 us; the launch traced here: 74 us
  matrix products  23.4 us (31%)
  waiting for transfers between devices  22.8 us (31%)
  starting transfers between devices  16.4 us (22%)
  other arithmetic  5.52 us (7%)
  local copies, waits for them, and re-layouts  5.14 us (7%)
  between operations  0.79 us (1%)
    ppermute x6, waiting for transfers between devices, partner(): return lax.ppermute(value, axis, pairs)  22.8 us
    dot_general x21, matrix products, complex_apply(): jnp.einsum('bri,bio->bro', values[..., half:], weights, precision=lax.Pre...  13.1 us
    dot_general x21, matrix products, complex_apply(): jnp.einsum('bri,bio->bro', values[..., :half], weights, precision=lax.Pre...  10.3 us
    ppermute x1, starting transfers between devices, padded(): lax.ppermute(lax.slice_in_dim(block, 0, width, axis=dim), axis, backward)  7.57 us
    ppermute x6, starting transfers between devices, partner(): return lax.ppermute(value, axis, pairs)  7.51 us
    slice x1, local copies, waits for them, and re-layouts, far_field(): weights = butterfly[level]  2.77 us
    sub x20, other arithmetic, complex_apply(): real_out = real_in[..., :width] - imag_in[..., width:]  2.52 us
    add x9, other arithmetic, far_field(): complex_apply(coef, weights[:, 0]) + complex_apply(other, weights[:, 1])  1.9 us
  transfers between devices with their start and end apart: 8, of which 4 were waited for; matrix products, arithmetic and copies ran while one was open for 21% of the time, Pallas kernels for 0%

commit v1 on v0

v1 whole, which is shorter than its diff:
```python
import jax
import jax.numpy as jnp
from jax import lax
from jax.sharding import PartitionSpec as P


def product(values, weights):
    return jnp.einsum("bri,bio->bro", values, weights, precision=lax.Precision.HIGH)


def turned(values):
    half = values.shape[-1] // 2
    return jnp.concatenate([-values[..., half:], values[..., :half]], axis=-1)


def expanded(weights):
    return jnp.concatenate([weights, turned(weights)], axis=-2)


def level_weights(weights):
    count, _, rank, width = weights.shape
    return expanded(weights).reshape(count, 4 * rank, width)


def stacked(values):
    half = values.shape[-1] // 2
    return jnp.concatenate([values[..., :half], values[..., half:]], axis=1)


def unstacked(values):
    half = values.shape[1] // 2
    return values[:, :half] + turned(values[:, half:])


def local_partner(coef, level):
    half = 2**level
    shaped = coef.reshape(coef.shape[0] // (2 * half), 2, half, coef.shape[1], coef.shape[2])
    return jnp.flip(shaped, 1).reshape(coef.shape)


def exchange(value, mask):
    pairs = [(source, source ^ mask) for source in range(lax.axis_size("box"))]
    return lax.ppermute(value, "box", pairs)


def on_device(rhs_block, near_blocks, near_mask, compress, butterfly, expand):
    count = rhs_block.shape[0]
    local_bits = count.bit_length() - 1
    levels = butterfly.shape[0]
    size = lax.axis_size("box")

    coef = product(rhs_block, expanded(compress))
    for level in range(local_bits):
        other = local_partner(coef, level)
        coef = product(jnp.concatenate([coef, other], -1), level_weights(butterfly[level]))

    forward = [(i, (i + 1) % size) for i in range(size)]
    backward = [(target, source) for source, target in forward]
    masks = near_mask.astype(jnp.float32)
    low = lax.ppermute(rhs_block[count - 1 :], "box", forward)
    high = lax.ppermute(rhs_block[:1], "box", backward)
    before = jnp.concatenate([low, rhs_block[:-1]], 0) * masks[0][:, None, None]
    after = jnp.concatenate([rhs_block[1:], high], 0) * masks[1][:, None, None]

    near = product(stacked(rhs_block), near_blocks[:, 1])
    near = near + product(stacked(before), near_blocks[:, 0])
    near = near + product(stacked(after), near_blocks[:, 2])
    near = unstacked(near)

    for level in range(local_bits, levels):
        other = exchange(coef, 2 ** (level - local_bits))
        coef = product(jnp.concatenate([coef, other], -1), level_weights(butterfly[level]))
    return near + product(coef, expanded(expand))


def solution(mesh):
    placed = (
        P("box", "rhs", None),
        P("box", None, None, None),
        P(None, "box"),
        P("box", None, None),
        P(None, "box", None, None, None),
        P("box", None, None),
    )
    return jax.shard_map(
        on_device, mesh=mesh, in_specs=placed, out_specs=P("box", "rhs", None), check_vma=False
    )
```

time: 74.3 us -> 58.6 us (0.79)
  matrix products: 23.4 us -> 6.43 us
  waiting for transfers between devices: 22.8 us -> 28 us
  local copies, waits for them, and re-layouts: 5.14 us -> 2.87 us
    dot_general x42 -> x13, matrix products: 23.4 us -> 6.43 us  [product(): jnp.einsum('bri,bio->bro', values, weights, precision=lax.Precision.HIGH)]
    ppermute x8, waiting for transfers between devices: 22.8 us -> 28 us  [the longest x6 27 us: exchange(): return lax.ppermute(value, 'box', pairs)]
    add x10 -> x0, other arithmetic: 2.9 us -> none  [the longest x9 1.9 us: far_field(): complex_apply(coef, weights[:, 0]) + complex_apply(other, weights[:, 1])]
    slice x2 -> x5, local copies, waits for them, and re-layouts: 2.79 us -> 0.19 us  [the longest x3 0.12 us: stacked(): return jnp.concatenate([values[..., :half], values[..., half:]], axis=1)]
    neg x0 -> x8, other arithmetic: none -> 2.56 us  [turned(): return jnp.concatenate([-values[..., half:], values[..., :half]], axis=-1)]
    sub x20 -> x0, other arithmetic: 2.52 us -> none  [complex_apply(): real_out = real_in[..., :width] - imag_in[..., width:]]
    concatenate x1 -> x7, other arithmetic: 0.1 us -> 2.18 us  [expanded(): return jnp.concatenate([weights, turned(weights)], axis=-2)]
  transfers between devices with their start and end apart: 8 -> 8, of which waited for: 4 -> 6; matrix products, arithmetic and copies ran while one was open for 21% -> 8% of each run, Pallas kernels for 0% -> 0%
where the time goes in v1:
time: 58.6 us; the launch traced here: 58.5 us
  waiting for transfers between devices  28 us (48%)
  starting transfers between devices  15.9 us (27%)
  matrix products  6.43 us (11%)
  other arithmetic  4.93 us (8%)
  local copies, waits for them, and re-layouts  2.87 us (5%)
    ppermute x6, waiting for transfers between devices, exchange(): return lax.ppermute(value, 'box', pairs)  27 us
    ppermute x1, starting transfers between devices, on_device(): high = lax.ppermute(rhs_block[:1], 'box', backward)  7.58 us
    ppermute x6, starting transfers between devices, exchange(): return lax.ppermute(value, 'box', pairs)  7.04 us
    dot_general x13, matrix products, product(): jnp.einsum('bri,bio->bro', values, weights, precision=lax.Precision.HIGH)  6.43 us
    neg x8, other arithmetic, turned(): return jnp.concatenate([-values[..., half:], values[..., :half]], axis=-1)  2.56 us
    concatenate x7, other arithmetic, expanded(): return jnp.concatenate([weights, turned(weights)], axis=-2)  2.18 us
    squeeze x1, local copies, waits for them, and re-layouts, on_device(): butterfly[level]  1.64 us
    ppermute x1, starting transfers between devices, on_device(): low = lax.ppermute(rhs_block[count - 1:], 'box', forward)  1.31 us
  transfers between devices with their start and end apart: 8, of which 6 were waited for; matrix products, arithmetic and copies ran while one was open for 8% of the time, Pallas kernels for 0%

profile of v1, /device:TPU:8, one launch (start us, length us, event | category | flops | bytes accessed | tf_op | source)
XLA Modules:
  0.0 58.5 jit_solution(15330325917241878057)
XLA Ops:
  0.0 1.6 %slice_bitcast_fusion.7 = (f32[4,2,64,128]{3,2,1,0:T(8,128)S(1)}, f32[4,2,64,128]{3,2,1,0:T(8,128)S(1)}, f32[4,2,64,128]{3,2,1,0:T(8,128)S(1)}, f32[4,2,64,128]{...) fusion(f32[8,4,2,64,128]{4,3,2,1,0:T(8,128)} %param.10), kind=kLoop, calls=%fused_computation.93 | loop fusion | bytes 4194304 | tf_op jit(solution)/shard_map/squeeze | solution.py:55
  1.7 0.8 %slice_negate_fusion.8 = (f32[4,2,64,64]{3,2,1,0:T(8,128)S(1)}, f32[4,2,64,64]{3,2,1,0:T(8,128)}) fusion(f32[4,2,64,128]{3,2,1,0:T(8,128)S(1)} %get-tuple-element.5), kind=kLoop, calls=%fused_computation.51 | loop fusion | flops 32768 | bytes 524288 | tf_op jit(solution)/shard_map/neg | solution.py:13
  2.4 0.9 %slice_negate_fusion.7 = (f32[4,2,64,64]{3,2,1,0:T(8,128)}, f32[4,2,64,64]{3,2,1,0:T(8,128)}) fusion(f32[4,2,64,128]{3,2,1,0:T(8,128)S(1)} %get-tuple-element.10), kind=kLoop, calls=%fused_computation.50 | loop fusion | flops 32768 | bytes 524288 | tf_op jit(solution)/shard_map/neg | solution.py:13
  3.5 0.5 fusion.15
  4.1 0.7 %rev.8 = f32[2,2,1,64,128]{4,3,1,0,2:T(8,128)} reverse(f32[2,2,1,64,128]{4,3,1,0,2:T(8,128)S(1)} %bitcast.73), dimensions={1} | reverse | bytes 262144 | tf_op jit(solution)/shard_map/jit(_flip)/rev | solution.py:38
  4.7 1.3 %maximum_maximum_fusion = (f32[4,2,128,128]{3,2,1,0:T(8,128)S(1)}, f32[4,2,128,128]{3,2,1,0:T(8,128)S(1)}) fusion(f32[4,2,64,64]{3,2,1,0:T(8,128)} %get-tuple-element.30, f32[4,2,64,64]{3,2,1,0:T(8,128)S(1)} %get-tuple-element.29, f32[4,2,64,128]{3,2,1,0:T(8,128)S(1)} %get-tuple-element.5, f32[4,2,64,64]{3,2,1,0:T(8,128)} %get-tuple-element.32, ...), kind=kLoop, calls=%fused_computation.35 | loop fusion | flops 524288 | bytes 2097152 | tf_op jit(solution)/shard_map/concatenate | solution.py:17
  6.1 0.3 fusion.35
  6.4 0.3 fusion.39
  6.7 2.4 %collective-permute-start.2 = (f32[4,64,128]{2,1,0:T(8,128)S(1)}, f32[4,64,128]{2,1,0:T(8,128)S(1)}, u32[]{:S(2)}, u32[]{:S(2)}) collective-permute-start(f32[4,64,128]{2,1,0:T(8,128)S(1)} %fusion.39), channel_id=1, source_target_pairs={{0,4},{4,0},{8,12},{12,8},{16,20},{20,16},{24,28},{28,24},{32,36},... | collective-permute-start | bytes 393224 | tf_op jit(solution)/shard_map/ppermute | solution.py:43
  9.1 1.3 %collective-permute-start = (f32[1,64,512]{2,1,0:T(8,128)S(1)}, f32[1,64,512]{2,1,0:T(8,128)S(1)}, u32[]{:S(2)}, u32[]{:S(2)}) collective-permute-start(f32[1,64,512]{2,1,0:T(8,128)S(1)} %get-tuple-element.19), channel_id=1, source_target_pairs={{0,4},{4,8},{8,12},{12,16},{16,20},{20,24},{24,28},{28,32},{32,36}... | collective-permute-start | bytes 393224 | tf_op jit(solution)/shard_map/ppermute | solution.py:60
  10.4 7.6 %collective-permute-start.1 = (f32[1,64,512]{2,1,0:T(8,128)S(1)}, f32[1,64,512]{2,1,0:T(8,128)S(1)}, u32[]{:S(2)}, u32[]{:S(2)}) collective-permute-start(f32[1,64,512]{2,1,0:T(8,128)S(1)} %get-tuple-element.20), channel_id=1, source_target_pairs={{4,0},{8,4},{12,8},{16,12},{20,16},{24,20},{28,24},{32,28},{36,32}... | collective-permute-start | bytes 393224 | tf_op jit(solution)/shard_map/ppermute | solution.py:61
  18.2 0.2 slice_negate_fusion.5
  19.2 0.2 slice_negate_fusion.1
  19.7 0.3 fusion.43
  20.1 1.0 %collective-permute-done = f32[1,64,512]{2,1,0:T(8,128)S(1)} collective-permute-done((f32[1,64,512]{2,1,0:T(8,128)S(1)}, f32[1,64,512]{2,1,0:T(8,128)S(1)}, u32[]{:S(2)}, u32[]{:S(2)}) %collective-permute-start) | collective-permute-done | bytes 131104 | tf_op jit(solution)/shard_map/ppermute | solution.py:60
  21.4 0.3 slice-done.1
  21.7 0.8 %fusion = f32[4,128,512]{2,1,0:T(8,128)S(1)} fusion(f32[4,3,256,512]{3,2,1,0:T(8,128)S(1)} %bitcast.64, f32[4,64,256]{2,1,0:T(8,128)S(1)} %get-tuple-element.24, f32[4,64,256]{2,1,0:T(8,128)S(1)} %get-tuple-element.23), kind=kOutput, calls=%fused_computation | convolution fusion | flops 402784256 | bytes 3670016 | tf_op jit(solution)/shard_map/bri,bio->bro/dot_general | solution.py:8
  22.5 2.6 %collective-permute-done.3 = f32[4,64,128]{2,1,0:T(8,128)S(1)} collective-permute-done((f32[4,64,128]{2,1,0:T(8,128)S(1)}, f32[4,64,128]{2,1,0:T(8,128)S(1)}, u32[]{:S(2)}, u32[]{:S(2)}) %collective-permute-start.3) | collective-permute-done | bytes 131104 | tf_op jit(solution)/shard_map/ppermute | solution.py:43
  25.1 0.3 fusion.47
  25.5 6.9 %collective-permute-done.4 = f32[4,64,128]{2,1,0:T(8,128)S(1)} collective-permute-done((f32[4,64,128]{2,1,0:T(8,128)S(1)}, f32[4,64,128]{2,1,0:T(8,128)S(1)}, u32[]{:S(2)}, u32[]{:S(2)}) %collective-permute-start.4) | collective-permute-done | bytes 131104 | tf_op jit(solution)/shard_map/ppermute | solution.py:43
  32.4 0.3 fusion.51
  32.7 4.1 %collective-permute-start.5 = (f32[4,64,128]{2,1,0:T(8,128)S(1)}, f32[4,64,128]{2,1,0:T(8,128)S(1)}, u32[]{:S(2)}, u32[]{:S(2)}) collective-permute-start(f32[4,64,128]{2,1,0:T(8,128)S(1)} %fusion.51), channel_id=1, source_target_pairs={{0,32},{4,36},{8,40},{12,44},{16,48},{20,52},{24,56},{28,60},{32,0... | collective-permute-start | bytes 393224 | tf_op jit(solution)/shard_map/ppermute | solution.py:43
  36.8 0.8 %fusion.2 = f32[4,128,512]{2,1,0:T(8,128)S(1)} fusion(f32[4,3,256,512]{3,2,1,0:T(8,128)S(1)} %bitcast.64, f32[4,64,256]{2,1,0:T(8,128)S(1)} %get-tuple-element.18, f32[4,64,256]{2,1,0:T(8,128)S(1)} %get-tuple-element.17), kind=kOutput, calls=%fused_computation.2 | convolution fusion | flops 402784256 | bytes 3670016 | tf_op jit(solution)/shard_map/bri,bio->bro/dot_general | solution.py:8
  37.6 6.1 %collective-permute-done.5 = f32[4,64,128]{2,1,0:T(8,128)S(1)} collective-permute-done((f32[4,64,128]{2,1,0:T(8,128)S(1)}, f32[4,64,128]{2,1,0:T(8,128)S(1)}, u32[]{:S(2)}, u32[]{:S(2)}) %collective-permute-start.5) | collective-permute-done | bytes 131104 | tf_op jit(solution)/shard_map/ppermute | solution.py:43
  43.7 0.3 fusion.55
  44.1 0.9 %fusion.12 = f32[4,128,512]{2,1,0:T(8,128)S(1)} fusion(f32[4,128,512]{2,1,0:T(8,128)S(1)} %fusion, f32[4,128,512]{2,1,0:T(8,128)S(1)} %fusion.2, f32[4,3,256,512]{3,2,1,0:T(8,128)S(1)} %bitcast.64, f32[4,64,256]{2,1,0:T(8,128)S(1)} %get-tuple-element.16, f32[4,64,256]{2,1,0:T(8,128)S(1)} %get-tuple-element.15), kind=kOutput, calls=%fused_computation.10 | convolution fusion | flops 403308544 | bytes 5767168 | tf_op jit(solution)/shard_map/bri,bio->bro/dot_general | solution.py:8
  44.9 5.2 %collective-permute-done.6 = f32[4,64,128]{2,1,0:T(8,128)S(1)} collective-permute-done((f32[4,64,128]{2,1,0:T(8,128)S(1)}, f32[4,64,128]{2,1,0:T(8,128)S(1)}, u32[]{:S(2)}, u32[]{:S(2)}) %collective-permute-start.6) | collective-permute-done | bytes 131104 | tf_op jit(solution)/shard_map/ppermute | solution.py:43
  50.1 0.3 fusion.59
  50.4 0.3 collective-permute-start.7
  50.7 6.2 %collective-permute-done.7 = f32[4,64,128]{2,1,0:T(8,128)S(1)} collective-permute-done((f32[4,64,128]{2,1,0:T(8,128)S(1)}, f32[4,64,128]{2,1,0:T(8,128)S(1)}, u32[]{:S(2)}, u32[]{:S(2)}) %collective-permute-start.7) | collective-permute-done | bytes 131104 | tf_op jit(solution)/shard_map/ppermute | solution.py:43
  57.0 0.3 fusion.63
  57.3 1.3 %convolution_add_fusion = f32[4,64,512]{2,1,0:T(8,128)} fusion(f32[4,64,128]{2,1,0:T(8,128)S(1)} %fusion.63, f32[4,64,256]{2,1,0:T(8,128)S(1)} %get-tuple-element.26, f32[4,64,256]{2,1,0:T(8,128)S(1)} %get-tuple-element.25, f32[4,64,512]{2,1,0:T(8,128)S(1)} %copy-done.2, f32[4,128,512]{2,1,0:T(8,128)S(1)} %fusion.12, ...), kind=kOutput, calls=%fused_computation.11 | convolution fusion | flops 101580800 | bytes 2752512 | tf_op jit(solution)/shard_map/bri,bio->bro/dot_general | solution.py:8
  (38 shorter events, 2.1 us)
Async XLA Ops:
  1.6 1.7 %copy-start.1 = (f32[4,256,128]{2,1,0:T(8,128)S(1)}, f32[4,256,128]{2,1,0:T(8,128)}, u32[]{:S(2)}) copy-start(f32[4,256,128]{2,1,0:T(8,128)} %param.9) | copy-start | bytes 1572868
  1.7 1.9 %copy-start = (f32[4,64,512]{2,1,0:T(8,128)S(1)}, f32[4,64,512]{2,1,0:T(8,128)}, u32[]{:S(2)}) copy-start(f32[4,64,512]{2,1,0:T(8,128)} %param.6) | copy-start | bytes 1572868
  4.7 1.4 %copy-start.3 = (f32[2,2,1,64,128]{4,3,1,0,2:T(8,128)S(1)}, f32[2,2,1,64,128]{4,3,1,0,2:T(8,128)}, u32[]{:S(2)}) copy-start(f32[2,2,1,64,128]{4,3,1,0,2:T(8,128)} %rev.8) | copy-start | bytes 393220
  6.4 11.7 %copy-start.4 = (s32[2,4]{1,0:T(2,128)S(1)}, s32[2,4]{1,0:T(2,128)}, u32[]{:S(2)}) copy-start(s32[2,4]{1,0:T(2,128)} %param.8) | copy-start | bytes 100
  6.4 11.7 %copy-start.2 = (f32[4,64,512]{2,1,0:T(8,128)S(1)}, f32[4,64,512]{2,1,0:T(8,128)}, u32[]{:S(2)}) copy-start(f32[4,64,512]{2,1,0:T(8,128)} %param.11) | copy-start | bytes 1572868
  6.7 13.0 %collective-permute-start.2 = (f32[4,64,128]{2,1,0:T(8,128)S(1)}, f32[4,64,128]{2,1,0:T(8,128)S(1)}, u32[]{:S(2)}, u32[]{:S(2)}) collective-permute-start(f32[4,64,128]{2,1,0:T(8,128)S(1)} %fusion.39), channel_id=1, source_target_pairs={{0,4},{4,0},{8,12},{12,8},{16,20},{20,16},{24,28},{28,24},{32,36},... | collective-permute-start | bytes 393224 | tf_op jit(solution)/shard_map/ppermute | solution.py:43
  9.1 12.0 %collective-permute-start = (f32[1,64,512]{2,1,0:T(8,128)S(1)}, f32[1,64,512]{2,1,0:T(8,128)S(1)}, u32[]{:S(2)}, u32[]{:S(2)}) collective-permute-start(f32[1,64,512]{2,1,0:T(8,128)S(1)} %get-tuple-element.19), channel_id=1, source_target_pairs={{0,4},{4,8},{8,12},{12,16},{16,20},{20,24},{24,28},{28,32},{32,36}... | collective-permute-start | bytes 393224 | tf_op jit(solution)/shard_map/ppermute | solution.py:60
  10.4 10.7 %collective-permute-start.1 = (f32[1,64,512]{2,1,0:T(8,128)S(1)}, f32[1,64,512]{2,1,0:T(8,128)S(1)}, u32[]{:S(2)}, u32[]{:S(2)}) collective-permute-start(f32[1,64,512]{2,1,0:T(8,128)S(1)} %get-tuple-element.20), channel_id=1, source_target_pairs={{4,0},{8,4},{12,8},{16,12},{20,16},{24,20},{28,24},{32,28},{36,32}... | collective-permute-start | bytes 393224 | tf_op jit(solution)/shard_map/ppermute | solution.py:61
  18.7 2.7 %slice-start = ((s8[6291456]{0:T(1024)(128)(4,1)}), s8[4194304]{0:T(1024)(128)(4,1)S(1)}, s32[]{:S(2)}) async-start(s8[6291456]{0:T(1024)(128)(4,1)} %bitcast.63), calls=%async_computation | async-start | bytes 8388608
  19.2 2.5 %slice-start.1 = ((s8[6291456]{0:T(1024)(128)(4,1)}), s8[2097152]{0:T(1024)(128)(4,1)S(1)}, s32[]{:S(2)}) async-start(s8[6291456]{0:T(1024)(128)(4,1)} %bitcast.63), calls=%async_computation.1 | async-start | bytes 4194304
  20.0 5.1 %collective-permute-start.3 = (f32[4,64,128]{2,1,0:T(8,128)S(1)}, f32[4,64,128]{2,1,0:T(8,128)S(1)}, u32[]{:S(2)}, u32[]{:S(2)}) collective-permute-start(f32[4,64,128]{2,1,0:T(8,128)S(1)} %fusion.43), channel_id=1, source_target_pairs={{0,8},{4,12},{8,0},{12,4},{16,24},{20,28},{24,16},{28,20},{32,40},... | collective-permute-start | bytes 393224 | tf_op jit(solution)/shard_map/ppermute | solution.py:43
  25.4 7.0 %collective-permute-start.4 = (f32[4,64,128]{2,1,0:T(8,128)S(1)}, f32[4,64,128]{2,1,0:T(8,128)S(1)}, u32[]{:S(2)}, u32[]{:S(2)}) collective-permute-start(f32[4,64,128]{2,1,0:T(8,128)S(1)} %fusion.47), channel_id=1, source_target_pairs={{0,16},{4,20},{8,24},{12,28},{16,0},{20,4},{24,8},{28,12},{32,48},... | collective-permute-start | bytes 393224 | tf_op jit(solution)/shard_map/ppermute | solution.py:43
  32.7 11.0 %collective-permute-start.5 = (f32[4,64,128]{2,1,0:T(8,128)S(1)}, f32[4,64,128]{2,1,0:T(8,128)S(1)}, u32[]{:S(2)}, u32[]{:S(2)}) collective-permute-start(f32[4,64,128]{2,1,0:T(8,128)S(1)} %fusion.51), channel_id=1, source_target_pairs={{0,32},{4,36},{8,40},{12,44},{16,48},{20,52},{24,56},{28,60},{32,0... | collective-permute-start | bytes 393224 | tf_op jit(solution)/shard_map/ppermute | solution.py:43
  44.0 6.2 %collective-permute-start.6 = (f32[4,64,128]{2,1,0:T(8,128)S(1)}, f32[4,64,128]{2,1,0:T(8,128)S(1)}, u32[]{:S(2)}, u32[]{:S(2)}) collective-permute-start(f32[4,64,128]{2,1,0:T(8,128)S(1)} %fusion.55), channel_id=1, source_target_pairs={{0,64},{4,68},{8,72},{12,76},{16,80},{20,84},{24,88},{28,92},{32,9... | collective-permute-start | bytes 393224 | tf_op jit(solution)/shard_map/ppermute | solution.py:43
  50.4 6.6 %collective-permute-start.7 = (f32[4,64,128]{2,1,0:T(8,128)S(1)}, f32[4,64,128]{2,1,0:T(8,128)S(1)}, u32[]{:S(2)}, u32[]{:S(2)}) collective-permute-start(f32[4,64,128]{2,1,0:T(8,128)S(1)} %fusion.59), channel_id=1, source_target_pairs={{0,128},{4,132},{8,136},{12,140},{16,144},{20,148},{24,152},{28,15... | collective-permute-start | bytes 393224 | tf_op jit(solution)/shard_map/ppermute | solution.py:43

commit v2 on v1

v2 whole, which is shorter than its diff:
```python
import jax
import jax.numpy as jnp
from jax import lax
from jax.experimental import pallas as pl
from jax.experimental.pallas import tpu as pltpu
from jax.sharding import PartitionSpec as P

VMEM = pl.BlockSpec(memory_space=pltpu.VMEM)
ANY = pl.BlockSpec(memory_space=pl.ANY)
SMALL = pltpu.CompilerParams(vmem_limit_bytes=8 << 20)
F32 = jnp.float32
BF16 = jnp.bfloat16


def in_vmem(value):
    return pltpu.with_memory_space_constraint(value, pltpu.VMEM)


def cost(us):
    return pl.CostEstimate(flops=int(us * 1e8), bytes_accessed=int(us * 1e6), transcendentals=0)


def turned(values):
    half = values.shape[-1] // 2
    return jnp.concatenate([-values[..., half:], values[..., :half]], axis=-1)


def split(value):
    high = value.astype(BF16)
    return high, (value - high.astype(F32)).astype(BF16)


def dot(left, right):
    return jnp.dot(left, right, preferred_element_type=F32)


def apply_split(values, high, low):
    rows = values.shape[0]
    first, second = split(values)
    both = dot(jnp.concatenate([first, second], axis=0), high)
    return both[:rows] + (both[rows:] + dot(first, low))


def complex_dot(values, weights):
    half = values.shape[-1] // 2
    rows = jnp.concatenate([values[:, :half], values[:, half:]], axis=0)
    high, low = split(weights)
    both = apply_split(rows, high, low)
    count = values.shape[0]
    return both[:count] + turned(both[count:])


def level_dot(own, other, weights):
    half = own.shape[-1] // 2
    real = jnp.concatenate([own[:, :half], other[:, :half]], axis=1)
    imag = jnp.concatenate([own[:, half:], other[:, half:]], axis=1)
    high, low = split(weights.reshape(2 * half, weights.shape[-1]))
    count = own.shape[0]
    both = apply_split(jnp.concatenate([real, imag], axis=0), high, low)
    return both[:count] + turned(both[count:])


def head_kernel(x_hbm, c_hbm, w_hbm, out, x_buf, c_buf, w_buf, sems):
    count = x_buf.shape[0]
    copies = []
    for b in range(count):
        copies.append(pltpu.make_async_copy(x_hbm.at[b], x_buf.at[b], sems.at[2 * b]))
        copies.append(pltpu.make_async_copy(c_hbm.at[b], c_buf.at[b], sems.at[2 * b + 1]))
    levels = w_buf.shape[0]
    last = [
        pltpu.make_async_copy(w_hbm.at[level], w_buf.at[level], sems.at[2 * count + level])
        for level in range(levels)
    ]
    for copy in copies + last:
        copy.start()
    coef = []
    for b in range(count):
        copies[2 * b].wait()
        copies[2 * b + 1].wait()
        coef.append(complex_dot(x_buf[b], c_buf[b]))
    for level in range(levels):
        last[level].wait()
        coef = [level_dot(coef[b], coef[b ^ (1 << level)], w_buf[level, b]) for b in range(count)]
    for b in range(count):
        out[b] = coef[b]


def head(x, compress, butterfly, levels):
    count, rows, _ = x.shape
    width = compress.shape[-1]
    return pl.pallas_call(
        head_kernel,
        out_shape=[pltpu.VMEM((count, rows, width), F32), pltpu.VMEM(x.shape, F32)],
        in_specs=[ANY, ANY, ANY],
        out_specs=[VMEM, VMEM],
        scratch_shapes=[
            pltpu.VMEM(compress.shape, F32),
            pltpu.VMEM((levels,) + butterfly.shape[1:], F32),
            pltpu.SemaphoreType.DMA((2 * count + levels,)),
        ],
        cost_estimate=cost(2.5),
        name="head",
    )(x, compress, butterfly)


def prepare_kernel(level, weights_ref, after, high, low):
    del after
    _, count, slots, rank, _ = weights_ref.shape
    for b in range(count):
        for s in range(slots):
            base = 2 * rank * s
            weights = weights_ref[level, b, s]
            high[b, base : base + rank], low[b, base : base + rank] = split(weights)
            base += rank
            high[b, base : base + rank], low[b, base : base + rank] = split(turned(weights))


def prepare(level, butterfly, after):
    _, count, slots, rank, width = butterfly.shape
    shape = pltpu.VMEM((count, 2 * slots * rank, width), BF16)
    return pl.pallas_call(
        lambda *refs: prepare_kernel(level, *refs),
        out_shape=[shape, shape],
        in_specs=[VMEM, VMEM],
        out_specs=[VMEM, VMEM],
        compiler_params=SMALL,
        cost_estimate=cost(0.25),
        name=f"prepare{level}",
    )(in_vmem(butterfly), in_vmem(after))


def prepare_expand_kernel(weights_ref, after, high, low):
    del after
    count, rank, _ = weights_ref.shape
    for b in range(count):
        weights = weights_ref[b]
        high[b, :rank], low[b, :rank] = split(weights)
        high[b, rank:], low[b, rank:] = split(turned(weights))


def prepare_expand(expand, after):
    count, rank, width = expand.shape
    shape = pltpu.VMEM((count, 2 * rank, width), BF16)
    return pl.pallas_call(
        prepare_expand_kernel,
        out_shape=[shape, shape],
        in_specs=[VMEM, VMEM],
        out_specs=[VMEM, VMEM],
        compiler_params=SMALL,
        cost_estimate=cost(0.25),
        name="prepare_expand",
    )(in_vmem(expand), in_vmem(after))


def level_kernel(own, other, high, low, *rest):
    out = rest[-1]
    for b in range(own.shape[0]):
        out[b] = apply_split(jnp.concatenate([own[b], other[b]], axis=1), high[b], low[b])


def level_step(own, other, high, low, name, *ties):
    values = (own, other, high, low) + ties
    return pl.pallas_call(
        level_kernel,
        out_shape=pltpu.VMEM(own.shape, F32),
        in_specs=[VMEM] * len(values),
        out_specs=VMEM,
        compiler_params=SMALL,
        cost_estimate=cost(0.25),
        name=name,
    )(*map(in_vmem, values))


def last_kernel(own, other, high, low, e_high, e_low, near, out_hbm, out_buf, sems):
    copies = []
    for b in range(own.shape[0]):
        coef = apply_split(jnp.concatenate([own[b], other[b]], axis=1), high[b], low[b])
        out_buf[b] = near[b] + apply_split(coef, e_high[b], e_low[b])
        copies.append(pltpu.make_async_copy(out_buf.at[b], out_hbm.at[b], sems.at[b]))
        copies[b].start()
    for copy in copies:
        copy.wait()


def last_step(own, other, high, low, e_high, e_low, near):
    return pl.pallas_call(
        last_kernel,
        out_shape=jax.ShapeDtypeStruct(near.shape, F32),
        in_specs=[VMEM] * 7,
        out_specs=ANY,
        scratch_shapes=[
            pltpu.VMEM(near.shape, F32),
            pltpu.SemaphoreType.DMA((near.shape[0],)),
        ],
        compiler_params=SMALL,
        cost_estimate=cost(1.0),
        name="last",
    )(*map(in_vmem, (own, other, high, low, e_high, e_low, near)))


def product(values, weights):
    return jnp.einsum("bri,bio->bro", values, weights, precision=lax.Precision.HIGH)


def stacked(values):
    half = values.shape[-1] // 2
    return jnp.concatenate([values[..., :half], values[..., half:]], axis=1)


def unstacked(values):
    half = values.shape[1] // 2
    return values[:, :half] + turned(values[:, half:])


def exchange(value, mask):
    pairs = [(source, source ^ mask) for source in range(lax.axis_size("box"))]
    return lax.ppermute(value, "box", pairs)


def after(value, other):
    return lax.optimization_barrier((value, other))[0]


def on_device(rhs_block, near_blocks, near_mask, compress, butterfly, expand):
    count = rhs_block.shape[0]
    local_bits = count.bit_length() - 1
    size = lax.axis_size("box")
    even = lax.axis_index("box") % 2 == 0
    masks = near_mask.astype(F32)

    def weights(level, coef):
        return prepare(level, butterfly, coef)

    coef, x = head(rhs_block, compress, butterfly, local_bits)
    first, final = x[:1], x[count - 1 :]
    pairs = [(i, (i - 1 if i % 2 == 0 else i + 1) % size) for i in range(size)]

    other = exchange(coef, 1)
    level2 = weights(2, coef)
    inner = exchange(after(jnp.where(even, final, first), level2[0]), 1)
    coef = level_step(coef, other, *level2, "level2")

    other = exchange(coef, 2)
    level3 = weights(3, coef)
    coef = level_step(coef, other, *level3, "level3", inner)

    other = exchange(coef, 4)
    level4 = weights(4, coef)
    near = product(stacked(after(x, level4[0])), near_blocks[:, 1])
    level5 = weights(5, coef)
    level6 = weights(6, coef)
    level7 = weights(7, coef)
    coef = level_step(coef, other, *level4, "level4", *level5, *level6, *level7, near)

    other = exchange(coef, 8)
    far = prepare_expand(expand, coef)
    outer = lax.ppermute(after(jnp.where(even, first, final), far[0]), "box", pairs)
    coef = level_step(coef, other, *level5, "level5")

    other = exchange(coef, 16)
    coef = level_step(coef, other, *level6, "level6")

    other = exchange(coef, 32)
    below = jnp.where(even, outer, inner)
    above = jnp.where(even, inner, outer)
    below, above, _ = lax.optimization_barrier((below, above, coef))
    before = jnp.concatenate([below, x[:-1]], 0) * masks[0][:, None, None]
    behind = jnp.concatenate([x[1:], above], 0) * masks[1][:, None, None]
    near = near + product(stacked(before), near_blocks[:, 0])
    near = near + product(stacked(behind), near_blocks[:, 2])
    return last_step(coef, other, *level7, *far, unstacked(near))


def solution(mesh):
    placed = (
        P("box", "rhs", None),
        P("box", None, None, None),
        P(None, "box"),
        P("box", None, None),
        P(None, "box", None, None, None),
        P("box", None, None),
    )
    return jax.shard_map(
        on_device, mesh=mesh, in_specs=placed, out_specs=P("box", "rhs", None), check_vma=False
    )
```

time: 58.6 us -> 52.5 us (0.90)
  the two profiles are of different devices: /device:TPU:8 before, /device:TPU:2 now
where the time goes in v2:
time: 52.5 us; the launch traced here: 52.4 us
  starting transfers between devices  26 us (50%)
  waiting for transfers between devices  13.3 us (25%)
  Pallas kernels  7.39 us (14%)
  matrix products  2.44 us (5%)
  local copies, waits for them, and re-layouts  1.8 us (3%)
  other arithmetic  1.24 us (2%)
    ppermute x7, starting transfers between devices, exchange(): return lax.ppermute(value, 'box', pairs)  20.3 us
    ppermute x7, waiting for transfers between devices, exchange(): return lax.ppermute(value, 'box', pairs)  12.5 us
    ppermute x1, starting transfers between devices, on_device(): lax.ppermute(after(jnp.where(even, first, final), far[0]), 'box', pairs)  5.68 us
    pallas_call x1, Pallas kernels, head(): pl.pallas_call(head_kernel, out_shape=[pltpu.VMEM((count, rows, width), F...  3.17 us
    dot_general x3, matrix products, product(): jnp.einsum('bri,bio->bro', values, weights, precision=lax.Precision.HIGH)  2.44 us
    pallas_call x1, Pallas kernels, last_step(): pl.pallas_call(last_kernel, out_shape=jax.ShapeDtypeStruct(near.shape, F3...  1.67 us
    unnamed x8, local copies, waits for them, and re-layouts  1.61 us
    pallas_call x5, Pallas kernels, level_step(): pl.pallas_call(level_kernel, out_shape=pltpu.VMEM(own.shape, F32), in_spe...  1.26 us
  transfers between devices with their start and end apart: 8, of which 7 were waited for; matrix products, arithmetic and copies ran while one was open for 7% of the time, Pallas kernels for 3%

profile of v2, /device:TPU:2, one launch (start us, length us, event | category | flops | bytes accessed | tf_op | source)
XLA Modules:
  0.0 52.4 jit_solution(3801170555359002011)
XLA Ops:
  0.0 3.2 %head.1 = (f32[4,64,128]{2,1,0:T(8,128)S(1)}, f32[4,64,512]{2,1,0:T(8,128)S(1)}) custom-call(f32[4,64,512]{2,1,0:T(8,128)} %x_hbm.1, f32[4,256,128]{2,1,0:T(8,128)} %c_hbm.1, f32[8,4,2,64,128]{4,3,2,1,0:T(8,128)} %refs_0_.11), custom_call_target="tpu_custom_call" | custom-call | flops 250000000 | bytes 2500000 | tf_op jit(solution)/shard_map/head/pallas_call | solution.py:91
  3.2 3.3 %collective-permute-start = (f32[4,64,128]{2,1,0:T(8,128)S(1)}, f32[4,64,128]{2,1,0:T(8,128)S(1)}, u32[]{:S(2)}, u32[]{:S(2)}) collective-permute-start(f32[4,64,128]{2,1,0:T(8,128)S(1)} %get-tuple-element.26.refs_1_.own), channel_id=1, source_target_pairs={{0,4},{4,0},{8,12},{12,8},{16,20},{20,16},{24,28},{28,24},{32,36},... | collective-permute-start | bytes 393224 | tf_op jit(solution)/shard_map/ppermute | solution.py:217
  6.5 1.6 %copy-done = f32[8,4,2,64,128]{4,3,2,1,0:T(8,128)S(1)} copy-done((f32[8,4,2,64,128]{4,3,2,1,0:T(8,128)S(1)}, f32[8,4,2,64,128]{4,3,2,1,0:T(8,128)}, u32[]{:S(2)}) %copy-start) | copy-done | bytes 2097176
  8.3 0.4 collective-permute-start.2
  8.7 0.9 %convert_element_type.3 = f32[2,4]{1,0:T(2,128)S(1)} convert(s32[2,4]{1,0:T(2,128)} %param.8) | non-fusion elementwise | flops 8 | bytes 64 | tf_op jit(solution)/shard_map/convert_element_type | solution.py:229
  9.6 0.4 collective-permute-done.other
  10.1 0.2 level2.1.refs_1_.own
  10.3 2.0 %collective-permute-start.1 = (f32[4,64,128]{2,1,0:T(8,128)S(1)}, f32[4,64,128]{2,1,0:T(8,128)S(1)}, u32[]{:S(2)}, u32[]{:S(2)}) collective-permute-start(f32[4,64,128]{2,1,0:T(8,128)S(1)} %level2.1.refs_1_.own), channel_id=1, source_target_pairs={{0,8},{4,12},{8,0},{12,4},{16,24},{20,28},{24,16},{28,20},{32,40},... | collective-permute-start | bytes 393224 | tf_op jit(solution)/shard_map/ppermute | solution.py:217
  12.4 0.2 prepare3.1
  12.6 2.3 %collective-permute-done.2.rest_0_ = f32[1,64,512]{2,1,0:T(8,128)S(1)} collective-permute-done((f32[1,64,512]{2,1,0:T(8,128)S(1)}, f32[1,64,512]{2,1,0:T(8,128)S(1)}, u32[]{:S(2)}, u32[]{:S(2)}) %collective-permute-start.2) | collective-permute-done | bytes 131104 | tf_op jit(solution)/shard_map/ppermute | solution.py:217
  14.9 0.5 collective-permute-done.1.other
  15.4 0.3 level3.1.refs_1_.own
  15.6 0.2 prepare4.1
  15.8 3.4 %collective-permute-start.3 = (f32[4,64,128]{2,1,0:T(8,128)S(1)}, f32[4,64,128]{2,1,0:T(8,128)S(1)}, u32[]{:S(2)}, u32[]{:S(2)}) collective-permute-start(f32[4,64,128]{2,1,0:T(8,128)S(1)} %level3.1.refs_1_.own), channel_id=1, source_target_pairs={{0,16},{4,20},{8,24},{12,28},{16,0},{20,4},{24,8},{28,12},{32,48},... | collective-permute-start | bytes 393224 | tf_op jit(solution)/shard_map/ppermute | solution.py:217
  19.3 0.8 %fusion.4.rest_6_ = f32[4,128,512]{2,1,0:T(8,128)S(1)} fusion(f32[4,3,256,512]{3,2,1,0:T(8,128)S(1)} %copy-done.3, f32[4,64,256]{2,1,0:T(8,128)S(1)} %get-tuple-element.58, f32[4,64,256]{2,1,0:T(8,128)S(1)} %get-tuple-element.57), kind=kOutput, calls=%fused_computation.4 | convolution fusion | flops 402784256 | bytes 3670016 | tf_op jit(solution)/shard_map/bri,bio->bro/dot_general | solution.py:202
  20.3 0.2 prepare6.1
  20.5 0.2 prepare7.1
  20.7 3.2 %collective-permute-done.3.other = f32[4,64,128]{2,1,0:T(8,128)S(1)} collective-permute-done((f32[4,64,128]{2,1,0:T(8,128)S(1)}, f32[4,64,128]{2,1,0:T(8,128)S(1)}, u32[]{:S(2)}, u32[]{:S(2)}) %collective-permute-start.3) | collective-permute-done | bytes 131104 | tf_op jit(solution)/shard_map/ppermute | solution.py:217
  23.9 0.3 level4.1.own.after
  24.2 6.7 %collective-permute-start.4 = (f32[4,64,128]{2,1,0:T(8,128)S(1)}, f32[4,64,128]{2,1,0:T(8,128)S(1)}, u32[]{:S(2)}, u32[]{:S(2)}) collective-permute-start(f32[4,64,128]{2,1,0:T(8,128)S(1)} %level4.1.own.after), channel_id=1, source_target_pairs={{0,32},{4,36},{8,40},{12,44},{16,48},{20,52},{24,56},{28,60},{32,0... | collective-permute-start | bytes 393224 | tf_op jit(solution)/shard_map/ppermute | solution.py:217
  30.9 5.7 %collective-permute-start.7 = (f32[1,64,512]{2,1,0:T(8,128)S(1)}, f32[1,64,512]{2,1,0:T(8,128)S(1)}, u32[]{:S(2)}, u32[]{:S(2)}) collective-permute-start(f32[1,64,512]{2,1,0:T(8,128)S(1)} %get-tuple-element.44), channel_id=1, source_target_pairs={{0,252},{4,8},{8,4},{12,16},{16,12},{20,24},{24,20},{28,32},{32,28... | collective-permute-start | bytes 393224 | tf_op jit(solution)/shard_map/ppermute | solution.py:257
  36.6 0.3 level5.1.own
  36.9 2.8 %collective-permute-start.5 = (f32[4,64,128]{2,1,0:T(8,128)S(1)}, f32[4,64,128]{2,1,0:T(8,128)S(1)}, u32[]{:S(2)}, u32[]{:S(2)}) collective-permute-start(f32[4,64,128]{2,1,0:T(8,128)S(1)} %level5.1.own), channel_id=1, source_target_pairs={{0,64},{4,68},{8,72},{12,76},{16,80},{20,84},{24,88},{28,92},{32,9... | collective-permute-start | bytes 393224 | tf_op jit(solution)/shard_map/ppermute | solution.py:217
  39.7 0.8 %collective-permute-done.7 = f32[1,64,512]{2,1,0:T(8,128)S(1)} collective-permute-done((f32[1,64,512]{2,1,0:T(8,128)S(1)}, f32[1,64,512]{2,1,0:T(8,128)S(1)}, u32[]{:S(2)}, u32[]{:S(2)}) %collective-permute-start.7) | collective-permute-done | bytes 131104 | tf_op jit(solution)/shard_map/ppermute | solution.py:257
  40.5 3.4 %collective-permute-done.5.other = f32[4,64,128]{2,1,0:T(8,128)S(1)} collective-permute-done((f32[4,64,128]{2,1,0:T(8,128)S(1)}, f32[4,64,128]{2,1,0:T(8,128)S(1)}, u32[]{:S(2)}, u32[]{:S(2)}) %collective-permute-start.5) | collective-permute-done | bytes 131104 | tf_op jit(solution)/shard_map/ppermute | solution.py:217
  43.9 0.3 level6.1.own
  44.2 1.8 %collective-permute-start.6 = (f32[4,64,128]{2,1,0:T(8,128)S(1)}, f32[4,64,128]{2,1,0:T(8,128)S(1)}, u32[]{:S(2)}, u32[]{:S(2)}) collective-permute-start(f32[4,64,128]{2,1,0:T(8,128)S(1)} %level6.1.own), channel_id=1, source_target_pairs={{0,128},{4,132},{8,136},{12,140},{16,144},{20,148},{24,152},{28,15... | collective-permute-start | bytes 393224 | tf_op jit(solution)/shard_map/ppermute | solution.py:217
  45.9 0.2 maximum_multiply_fusion
  46.2 0.8 %fusion = f32[4,128,512]{2,1,0:T(8,128)S(1)} fusion(f32[4,3,256,512]{3,2,1,0:T(8,128)S(1)} %copy-done.3, f32[4,64,256]{2,1,0:T(8,128)S(1)} %get-tuple-element.54, f32[4,64,256]{2,1,0:T(8,128)S(1)} %get-tuple-element.53), kind=kOutput, calls=%fused_computation | convolution fusion | flops 402784256 | bytes 3670016 | tf_op jit(solution)/shard_map/bri,bio->bro/dot_general | solution.py:202
  47.0 0.9 %fusion.12 = f32[4,128,512]{2,1,0:T(8,128)S(1)} fusion(f32[4,128,512]{2,1,0:T(8,128)S(1)} %fusion, f32[4,128,512]{2,1,0:T(8,128)S(1)} %fusion.4.rest_6_, f32[4,3,256,512]{3,2,1,0:T(8,128)S(1)} %copy-done.3, f32[4,64,256]{2,1,0:T(8,128)S(1)} %get-tuple-element.50, f32[4,64,256]{2,1,0:T(8,128)S(1)} %get-tuple-element.49), kind=kOutput, calls=%fused_computation.10 | convolution fusion | flops 403308544 | bytes 5767168 | tf_op jit(solution)/shard_map/bri,bio->bro/dot_general | solution.py:202
  48.0 2.7 %collective-permute-done.6.other = f32[4,64,128]{2,1,0:T(8,128)S(1)} collective-permute-done((f32[4,64,128]{2,1,0:T(8,128)S(1)}, f32[4,64,128]{2,1,0:T(8,128)S(1)}, u32[]{:S(2)}, u32[]{:S(2)}) %collective-permute-start.6) | collective-permute-done | bytes 131104 | tf_op jit(solution)/shard_map/ppermute | solution.py:217
  50.7 1.7 %last.1 = f32[4,64,512]{2,1,0:T(8,128)} custom-call(f32[4,64,128]{2,1,0:T(8,128)S(1)} %level6.1.own, f32[4,64,128]{2,1,0:T(8,128)S(1)} %collective-permute-done.6.other, bf16[4,256,128]{2,1,0:T(8,128)(2,1)S(1)} %get-tuple-element.39.rest_4_.high, bf16[4,256,128]{2,1,0:T(8,128)(2,1)S(1)} %get-tuple-element.40.rest_5_.low, ...), custom_call_target="tpu_custom_call" | custom-call | flops 100000000 | bytes 1000000 | tf_op jit(solution)/shard_map/last/pallas_call | solution.py:186
  (20 shorter events, 0.9 us)
Async XLA Ops:
  0.0 12.4 %copy-start.1 = (f32[8,4,2,64,128]{4,3,2,1,0:T(8,128)S(1)}, f32[8,4,2,64,128]{4,3,2,1,0:T(8,128)}, u32[]{:S(2)}) copy-start(f32[8,4,2,64,128]{4,3,2,1,0:T(8,128)} %refs_0_.11) | copy-start | bytes 6291460
  3.2 6.9 %collective-permute-start = (f32[4,64,128]{2,1,0:T(8,128)S(1)}, f32[4,64,128]{2,1,0:T(8,128)S(1)}, u32[]{:S(2)}, u32[]{:S(2)}) collective-permute-start(f32[4,64,128]{2,1,0:T(8,128)S(1)} %get-tuple-element.26.refs_1_.own), channel_id=1, source_target_pairs={{0,4},{4,0},{8,12},{12,8},{16,20},{20,16},{24,28},{28,24},{32,36},... | collective-permute-start | bytes 393224 | tf_op jit(solution)/shard_map/ppermute | solution.py:217
  6.5 1.6 %copy-start = (f32[8,4,2,64,128]{4,3,2,1,0:T(8,128)S(1)}, f32[8,4,2,64,128]{4,3,2,1,0:T(8,128)}, u32[]{:S(2)}) copy-start(f32[8,4,2,64,128]{4,3,2,1,0:T(8,128)} %refs_0_.11) | copy-start | bytes 6291460
  8.3 11.0 %copy-start.3 = (f32[4,3,256,512]{3,2,1,0:T(8,128)S(1)}, f32[4,3,256,512]{3,2,1,0:T(8,128)}, u32[]{:S(2)}) copy-start(f32[4,3,256,512]{3,2,1,0:T(8,128)} %param.7) | copy-start | bytes 18874372
  8.3 6.6 %collective-permute-start.2 = (f32[1,64,512]{2,1,0:T(8,128)S(1)}, f32[1,64,512]{2,1,0:T(8,128)S(1)}, u32[]{:S(2)}, u32[]{:S(2)}) collective-permute-start(f32[1,64,512]{2,1,0:T(8,128)S(1)} %get-tuple-element.32), channel_id=1, source_target_pairs={{0,4},{4,0},{8,12},{12,8},{16,20},{20,16},{24,28},{28,24},{32,36},... | collective-permute-start | bytes 393224 | tf_op jit(solution)/shard_map/ppermute | solution.py:217
  10.3 5.1 %collective-permute-start.1 = (f32[4,64,128]{2,1,0:T(8,128)S(1)}, f32[4,64,128]{2,1,0:T(8,128)S(1)}, u32[]{:S(2)}, u32[]{:S(2)}) collective-permute-start(f32[4,64,128]{2,1,0:T(8,128)S(1)} %level2.1.refs_1_.own), channel_id=1, source_target_pairs={{0,8},{4,12},{8,0},{12,4},{16,24},{20,28},{24,16},{28,20},{32,40},... | collective-permute-start | bytes 393224 | tf_op jit(solution)/shard_map/ppermute | solution.py:217
  15.8 8.1 %collective-permute-start.3 = (f32[4,64,128]{2,1,0:T(8,128)S(1)}, f32[4,64,128]{2,1,0:T(8,128)S(1)}, u32[]{:S(2)}, u32[]{:S(2)}) collective-permute-start(f32[4,64,128]{2,1,0:T(8,128)S(1)} %level3.1.refs_1_.own), channel_id=1, source_target_pairs={{0,16},{4,20},{8,24},{12,28},{16,0},{20,4},{24,8},{28,12},{32,48},... | collective-permute-start | bytes 393224 | tf_op jit(solution)/shard_map/ppermute | solution.py:217
  19.2 11.6 %copy-start.2 = (f32[4,64,512]{2,1,0:T(8,128)S(1)}, f32[4,64,512]{2,1,0:T(8,128)}, u32[]{:S(2)}) copy-start(f32[4,64,512]{2,1,0:T(8,128)} %weights_ref.1) | copy-start | bytes 1572868
  24.2 12.5 %collective-permute-start.4 = (f32[4,64,128]{2,1,0:T(8,128)S(1)}, f32[4,64,128]{2,1,0:T(8,128)S(1)}, u32[]{:S(2)}, u32[]{:S(2)}) collective-permute-start(f32[4,64,128]{2,1,0:T(8,128)S(1)} %level4.1.own.after), channel_id=1, source_target_pairs={{0,32},{4,36},{8,40},{12,44},{16,48},{20,52},{24,56},{28,60},{32,0... | collective-permute-start | bytes 393224 | tf_op jit(solution)/shard_map/ppermute | solution.py:217
  30.9 9.6 %collective-permute-start.7 = (f32[1,64,512]{2,1,0:T(8,128)S(1)}, f32[1,64,512]{2,1,0:T(8,128)S(1)}, u32[]{:S(2)}, u32[]{:S(2)}) collective-permute-start(f32[1,64,512]{2,1,0:T(8,128)S(1)} %get-tuple-element.44), channel_id=1, source_target_pairs={{0,252},{4,8},{8,4},{12,16},{16,12},{20,24},{24,20},{28,32},{32,28... | collective-permute-start | bytes 393224 | tf_op jit(solution)/shard_map/ppermute | solution.py:257
  36.9 7.0 %collective-permute-start.5 = (f32[4,64,128]{2,1,0:T(8,128)S(1)}, f32[4,64,128]{2,1,0:T(8,128)S(1)}, u32[]{:S(2)}, u32[]{:S(2)}) collective-permute-start(f32[4,64,128]{2,1,0:T(8,128)S(1)} %level5.1.own), channel_id=1, source_target_pairs={{0,64},{4,68},{8,72},{12,76},{16,80},{20,84},{24,88},{28,92},{32,9... | collective-permute-start | bytes 393224 | tf_op jit(solution)/shard_map/ppermute | solution.py:217
  44.2 6.6 %collective-permute-start.6 = (f32[4,64,128]{2,1,0:T(8,128)S(1)}, f32[4,64,128]{2,1,0:T(8,128)S(1)}, u32[]{:S(2)}, u32[]{:S(2)}) collective-permute-start(f32[4,64,128]{2,1,0:T(8,128)S(1)} %level6.1.own), channel_id=1, source_target_pairs={{0,128},{4,132},{8,136},{12,140},{16,144},{20,148},{24,152},{28,15... | collective-permute-start | bytes 393224 | tf_op jit(solution)/shard_map/ppermute | solution.py:217

commit v3 on v2

--- a/solution.py
+++ b/solution.py
@@ -129,27 +129,80 @@
     )(in_vmem(butterfly), in_vmem(after))
 
 
-def prepare_expand_kernel(weights_ref, after, high, low):
+def store_expanded(high, low, where, weights):
+    rank = weights.shape[0]
+    high[(*where, slice(0, rank))], low[(*where, slice(0, rank))] = split(weights)
+    weights = turned(weights)
+    high[(*where, slice(rank, None))], low[(*where, slice(rank, None))] = split(weights)
+
+
+def fuse_last_kernel(weights_ref, expand_ref, after, high, low):
     del after
-    count, rank, _ = weights_ref.shape
-    for b in range(count):
-        weights = weights_ref[b]
-        high[b, :rank], low[b, :rank] = split(weights)
-        high[b, rank:], low[b, rank:] = split(turned(weights))
-
-
-def prepare_expand(expand, after):
-    count, rank, width = expand.shape
-    shape = pltpu.VMEM((count, 2 * rank, width), BF16)
-    return pl.pallas_call(
-        prepare_expand_kernel,
+    level = weights_ref.shape[0] - 1
+    _, count, slots, rank, width = weights_ref.shape
+    for b in range(count):
+        expand = expand_ref[b]
+        expand = jnp.concatenate([expand, turned(expand)], axis=0)
+        both = apply_split(weights_ref[level, b].reshape(slots * rank, width), *split(expand))
+        for s in range(slots):
+            store_expanded(high, low, (b, s), both[s * rank : (s + 1) * rank])
+
+
+def fuse_last(butterfly, expand, after):
+    _, count, slots, rank, width = butterfly.shape
+    shape = pltpu.VMEM((count, slots, width, expand.shape[-1]), BF16)
+    return pl.pallas_call(
+        fuse_last_kernel,
         out_shape=[shape, shape],
-        in_specs=[VMEM, VMEM],
-        out_specs=[VMEM, VMEM],
-        compiler_params=SMALL,
-        cost_estimate=cost(0.25),
-        name="prepare_expand",
-    )(in_vmem(expand), in_vmem(after))
+        in_specs=[VMEM] * 3,
+        out_specs=[VMEM] * 2,
+        compiler_params=SMALL,
+        cost_estimate=cost(1.0),
+        name="fuse_last",
+    )(*map(in_vmem, (butterfly, expand, after)))
+
+
+def fuse_two_kernel(weights_ref, fetched_ref, m_high, m_low, after, high, low):
+    del after
+    level = weights_ref.shape[0] - 2
+    _, count, slots, rank, width = weights_ref.shape
+    for b in range(count):
+        for half, weights in enumerate((weights_ref[level, b], fetched_ref[0, b])):
+            rows = weights.reshape(slots * rank, width)
+            both = apply_split(rows, m_high[b, half], m_low[b, half])
+            for s in range(slots):
+                store_expanded(high, low, (b, 2 * half + s), both[s * rank : (s + 1) * rank])
+
+
+def fuse_two(butterfly, fetched, m_high, m_low, after):
+    count, slots, width, out = m_high.shape
+    shape = pltpu.VMEM((count, 2 * slots, width, out), BF16)
+    return pl.pallas_call(
+        fuse_two_kernel,
+        out_shape=[shape, shape],
+        in_specs=[VMEM] * 5,
+        out_specs=[VMEM] * 2,
+        compiler_params=SMALL,
+        cost_estimate=cost(1.5),
+        name="fuse_two",
+    )(*map(in_vmem, (butterfly, fetched, m_high, m_low, after)))
+
+
+def add_part_kernel(slot, near, coef, high, low, out):
+    for b in range(near.shape[0]):
+        out[b] = near[b] + apply_split(coef[b], high[b, slot], low[b, slot])
+
+
+def add_part(slot, *values):
+    return pl.pallas_call(
+        lambda *refs: add_part_kernel(slot, *refs),
+        out_shape=pltpu.VMEM(values[0].shape, F32),
+        in_specs=[VMEM] * 4,
+        out_specs=VMEM,
+        compiler_params=SMALL,
+        cost_estimate=cost(0.5),
+        name=f"part{slot}",
+    )(*map(in_vmem, values))
 
 
 def level_kernel(own, other, high, low, *rest):
@@ -171,22 +224,26 @@
     )(*map(in_vmem, values))
 
 
-def last_kernel(own, other, high, low, e_high, e_low, near, out_hbm, out_buf, sems):
+def last_kernel(two, both, high, low, near, out_hbm, out_buf, sems):
+    count = two.shape[0]
+    rows = 2 * high.shape[2]
     copies = []
-    for b in range(own.shape[0]):
-        coef = apply_split(jnp.concatenate([own[b], other[b]], axis=1), high[b], low[b])
-        out_buf[b] = near[b] + apply_split(coef, e_high[b], e_low[b])
+    for b in range(count):
+        coef = jnp.concatenate([two[b], both[b]], axis=1)
+        weights = (part[b, 2:].reshape(rows, part.shape[-1]) for part in (high, low))
+        out_buf[b] = near[b] + apply_split(coef, *weights)
         copies.append(pltpu.make_async_copy(out_buf.at[b], out_hbm.at[b], sems.at[b]))
         copies[b].start()
     for copy in copies:
         copy.wait()
 
 
-def last_step(own, other, high, low, e_high, e_low, near):
+def last_step(*values):
+    near = values[-1]
     return pl.pallas_call(
         last_kernel,
         out_shape=jax.ShapeDtypeStruct(near.shape, F32),
-        in_specs=[VMEM] * 7,
+        in_specs=[VMEM] * len(values),
         out_specs=ANY,
         scratch_shapes=[
             pltpu.VMEM(near.shape, F32),
@@ -195,7 +252,7 @@
         compiler_params=SMALL,
         cost_estimate=cost(1.0),
         name="last",
-    )(*map(in_vmem, (own, other, high, low, e_high, e_low, near)))
+    )(*map(in_vmem, values))
 
 
 def product(values, weights):
@@ -237,38 +294,39 @@
 
     other = exchange(coef, 1)
     level2 = weights(2, coef)
-    inner = exchange(after(jnp.where(even, final, first), level2[0]), 1)
     coef = level_step(coef, other, *level2, "level2")
 
     other = exchange(coef, 2)
     level3 = weights(3, coef)
-    coef = level_step(coef, other, *level3, "level3", inner)
+    inner = exchange(after(jnp.where(even, final, first), level3[0]), 1)
+    coef = level_step(coef, other, *level3, "level3")
 
     other = exchange(coef, 4)
     level4 = weights(4, coef)
+    fetched = exchange(after(butterfly[6:7], level4[0]), 32)
     near = product(stacked(after(x, level4[0])), near_blocks[:, 1])
     level5 = weights(5, coef)
-    level6 = weights(6, coef)
-    level7 = weights(7, coef)
-    coef = level_step(coef, other, *level4, "level4", *level5, *level6, *level7, near)
+    last = fuse_last(butterfly, expand, level4[0])
+    coef = level_step(coef, other, *level4, "level4", *level5, *last, near, inner)
 
     other = exchange(coef, 8)
-    far = prepare_expand(expand, coef)
-    outer = lax.ppermute(after(jnp.where(even, first, final), far[0]), "box", pairs)
-    coef = level_step(coef, other, *level5, "level5")
-
-    other = exchange(coef, 16)
-    coef = level_step(coef, other, *level6, "level6")
-
-    other = exchange(coef, 32)
+    fused = fuse_two(butterfly, fetched, *last, coef)
+    outer = lax.ppermute(after(jnp.where(even, first, final), fused[0]), "box", pairs)
+    coef = level_step(coef, other, *level5, "level5", *fused)
+
+    two = exchange(coef, 32)
+    both = exchange(coef, 48)
+    one = exchange(coef, 16)
     below = jnp.where(even, outer, inner)
     above = jnp.where(even, inner, outer)
     below, above, _ = lax.optimization_barrier((below, above, coef))
     before = jnp.concatenate([below, x[:-1]], 0) * masks[0][:, None, None]
     behind = jnp.concatenate([x[1:], above], 0) * masks[1][:, None, None]
     near = near + product(stacked(before), near_blocks[:, 0])
-    near = near + product(stacked(behind), near_blocks[:, 2])
-    return last_step(coef, other, *level7, *far, unstacked(near))
+    near = unstacked(near + product(stacked(behind), near_blocks[:, 2]))
+    near = add_part(0, near, coef, *fused)
+    near = add_part(1, near, one, *fused)
+    return last_step(two, both, *fused, near)
 
 
 def solution(mesh):

time: 52.5 us -> 47.5 us (0.905)
  the two profiles are of different devices: /device:TPU:2 before, /device:TPU:8 now
where the time goes in v3:
time: 47.5 us; the launch traced here: 46.8 us
  starting transfers between devices  29 us (61%)
  Pallas kernels  8.43 us (18%)
  waiting for transfers between devices  5.15 us (11%)
  matrix products  2.44 us (5%)
  local copies, waits for them, and re-layouts  0.97 us (2%)
    ppermute x9, starting transfers between devices, exchange(): return lax.ppermute(value, 'box', pairs)  24.5 us
    ppermute x1, starting transfers between devices, on_device(): lax.ppermute(after(jnp.where(even, first, final), fused[0]), 'box', pairs)  4.5 us
    ppermute x9, waiting for transfers between devices, exchange(): return lax.ppermute(value, 'box', pairs)  3.86 us
    pallas_call x1, Pallas kernels, head(): pl.pallas_call(head_kernel, out_shape=[pltpu.VMEM((count, rows, width), F...  3.17 us
    dot_general x3, matrix products, product(): jnp.einsum('bri,bio->bro', values, weights, precision=lax.Precision.HIGH)  2.44 us
    ppermute x1, waiting for transfers between devices, on_device(): lax.ppermute(after(jnp.where(even, first, final), fused[0]), 'box', pairs)  1.29 us
    pallas_call x1, Pallas kernels, last_step(): pl.pallas_call(last_kernel, out_shape=jax.ShapeDtypeStruct(near.shape, F3...  1.17 us
    pallas_call x4, Pallas kernels, level_step(): pl.pallas_call(level_kernel, out_shape=pltpu.VMEM(own.shape, F32), in_spe...  1.01 us
  transfers between devices with their start and end apart: 10, of which 3 were waited for; matrix products, arithmetic and copies ran while one was open for 8% of the time, Pallas kernels for 8%

profile of v3, /device:TPU:8, one launch (start us, length us, event | category | flops | bytes accessed | tf_op | source)
XLA Modules:
  0.0 46.8 jit_solution(12052156714860866799)
XLA Ops:
  0.0 3.2 %head.1 = (f32[4,64,128]{2,1,0:T(8,128)S(1)}, f32[4,64,512]{2,1,0:T(8,128)S(1)}) custom-call(f32[4,64,512]{2,1,0:T(8,128)} %x_hbm.1, f32[4,256,128]{2,1,0:T(8,128)} %c_hbm.1, f32[8,4,2,64,128]{4,3,2,1,0:T(8,128)} %weights_ref.3), custom_call_target="tpu_custom_call" | custom-call | flops 250000000 | bytes 2500000 | tf_op jit(solution)/shard_map/head/pallas_call | solution.py:91
  3.2 2.4 %collective-permute-start = (f32[4,64,128]{2,1,0:T(8,128)S(1)}, f32[4,64,128]{2,1,0:T(8,128)S(1)}, u32[]{:S(2)}, u32[]{:S(2)}) collective-permute-start(f32[4,64,128]{2,1,0:T(8,128)S(1)} %get-tuple-element.25.refs_1_.own), channel_id=1, source_target_pairs={{0,4},{4,0},{8,12},{12,8},{16,20},{20,16},{24,28},{28,24},{32,36},... | collective-permute-start | bytes 393224 | tf_op jit(solution)/shard_map/ppermute | solution.py:274
  5.6 0.2 prepare2.1
  5.8 0.7 %slice.65 = f32[1,4,2,64,128]{4,3,2,1,0:T(8,128)} slice(f32[8,4,2,64,128]{4,3,2,1,0:T(8,128)S(1)} %copy-done), slice={[6:7], [0:4], [0:2], [0:64], [0:128]} | slice | bytes 524288 | tf_op jit(solution)/shard_map/slice | solution.py:306
  6.6 3.4 %collective-permute-done.other = f32[4,64,128]{2,1,0:T(8,128)S(1)} collective-permute-done((f32[4,64,128]{2,1,0:T(8,128)S(1)}, f32[4,64,128]{2,1,0:T(8,128)S(1)}, u32[]{:S(2)}, u32[]{:S(2)}) %collective-permute-start) | collective-permute-done | bytes 131104 | tf_op jit(solution)/shard_map/ppermute | solution.py:274
  10.0 0.2 level2.1.refs_1_.own
  10.3 2.0 %collective-permute-start.1 = (f32[4,64,128]{2,1,0:T(8,128)S(1)}, f32[4,64,128]{2,1,0:T(8,128)S(1)}, u32[]{:S(2)}, u32[]{:S(2)}) collective-permute-start(f32[4,64,128]{2,1,0:T(8,128)S(1)} %level2.1.refs_1_.own), channel_id=1, source_target_pairs={{0,8},{4,12},{8,0},{12,4},{16,24},{20,28},{24,16},{28,20},{32,40},... | collective-permute-start | bytes 393224 | tf_op jit(solution)/shard_map/ppermute | solution.py:274
  12.3 0.2 prepare3.1
  12.5 2.4 %collective-permute-start.3 = (f32[1,64,512]{2,1,0:T(8,128)S(1)}, f32[1,64,512]{2,1,0:T(8,128)S(1)}, u32[]{:S(2)}, u32[]{:S(2)}) collective-permute-start(f32[1,64,512]{2,1,0:T(8,128)S(1)} %get-tuple-element.38), channel_id=1, source_target_pairs={{0,4},{4,0},{8,12},{12,8},{16,20},{20,16},{24,28},{28,24},{32,36},... | collective-permute-start | bytes 393224 | tf_op jit(solution)/shard_map/ppermute | solution.py:274
  14.9 0.4 collective-permute-done.1.other
  15.3 0.3 level3.1.refs_1_.own
  15.6 0.2 prepare4.1
  15.8 3.4 %collective-permute-start.2 = (f32[4,64,128]{2,1,0:T(8,128)S(1)}, f32[4,64,128]{2,1,0:T(8,128)S(1)}, u32[]{:S(2)}, u32[]{:S(2)}) collective-permute-start(f32[4,64,128]{2,1,0:T(8,128)S(1)} %level3.1.refs_1_.own), channel_id=1, source_target_pairs={{0,16},{4,20},{8,24},{12,28},{16,0},{20,4},{24,8},{28,12},{32,48},... | collective-permute-start | bytes 393224 | tf_op jit(solution)/shard_map/ppermute | solution.py:274
  19.2 3.1 %collective-permute-start.5 = (f32[1,4,2,64,128]{4,3,2,1,0:T(8,128)S(1)}, f32[1,4,2,64,128]{4,3,2,1,0:T(8,128)S(1)}, u32[]{:S(2)}, u32[]{:S(2)}) collective-permute-start(f32[1,4,2,64,128]{4,3,2,1,0:T(8,128)S(1)} %copy-done.3), channel_id=1, source_target_pairs={{0,128},{4,132},{8,136},{12,140},{16,144},{20,148},{24,152},{28,15... | collective-permute-start | bytes 786440 | tf_op jit(solution)/shard_map/ppermute | solution.py:274
  22.3 0.8 %fusion.4.rest_4_ = f32[4,128,512]{2,1,0:T(8,128)S(1)} fusion(f32[4,3,256,512]{3,2,1,0:T(8,128)S(1)} %copy-done.2, f32[4,64,256]{2,1,0:T(8,128)S(1)} %get-tuple-element.56, f32[4,64,256]{2,1,0:T(8,128)S(1)} %get-tuple-element.55), kind=kOutput, calls=%fused_computation.4 | convolution fusion | flops 402784256 | bytes 3670016 | tf_op jit(solution)/shard_map/bri,bio->bro/dot_general | solution.py:259
  23.1 0.2 prepare5.1
  23.4 0.6 %fuse_last.1 = (bf16[4,2,128,512]{3,2,1,0:T(8,128)(2,1)S(1)}, bf16[4,2,128,512]{3,2,1,0:T(8,128)(2,1)S(1)}) custom-call(f32[8,4,2,64,128]{4,3,2,1,0:T(8,128)S(1)} %copy-done, f32[4,64,512]{2,1,0:T(8,128)S(1)} %copy-done.1, bf16[4,256,128]{2,1,0:T(8,128)(2,1)S(1)} %get-tuple-element.30.after.high), custom_call_target="tpu_custom_call" | custom-call | flops 100000000 | bytes 1000000 | tf_op jit(solution)/shard_map/fuse_last/pallas_call | solution.py:154
  24.0 0.3 level4.1.after.own
  24.2 6.5 %collective-permute-start.4 = (f32[4,64,128]{2,1,0:T(8,128)S(1)}, f32[4,64,128]{2,1,0:T(8,128)S(1)}, u32[]{:S(2)}, u32[]{:S(2)}) collective-permute-start(f32[4,64,128]{2,1,0:T(8,128)S(1)} %level4.1.after.own), channel_id=1, source_target_pairs={{0,32},{4,36},{8,40},{12,44},{16,48},{20,52},{24,56},{28,60},{32,0... | collective-permute-start | bytes 393224 | tf_op jit(solution)/shard_map/ppermute | solution.py:274
  30.7 1.0 %fuse_two.1 = (bf16[4,4,128,512]{3,2,1,0:T(8,128)(2,1)S(1)}, bf16[4,4,128,512]{3,2,1,0:T(8,128)(2,1)S(1)}) custom-call(f32[8,4,2,64,128]{4,3,2,1,0:T(8,128)S(1)} %copy-done, f32[1,4,2,64,128]{4,3,2,1,0:T(8,128)S(1)} %collective-permute-done.5.fetched_ref, bf16[4,2,128,512]{3,2,1,0:T(8,128)(2,1)S(1)} %get-tuple-element.34.rest_2_.m_high, ...), custom_call_target="tpu_custom_call" | custom-call | flops 150000000 | bytes 1500000 | tf_op jit(solution)/shard_map/fuse_two/pallas_call | solution.py:180
  31.7 4.5 %collective-permute-start.8 = (f32[1,64,512]{2,1,0:T(8,128)S(1)}, f32[1,64,512]{2,1,0:T(8,128)S(1)}, u32[]{:S(2)}, u32[]{:S(2)}) collective-permute-start(f32[1,64,512]{2,1,0:T(8,128)S(1)} %get-tuple-element.42), channel_id=1, source_target_pairs={{0,252},{4,8},{8,4},{12,16},{16,12},{20,24},{24,20},{28,32},{32,28... | collective-permute-start | bytes 393224 | tf_op jit(solution)/shard_map/ppermute | solution.py:314
  36.2 0.3 level5.1.refs_1_
  36.5 0.1 collective-permute-start.9
  36.6 2.3 %collective-permute-start.6 = (f32[4,64,128]{2,1,0:T(8,128)S(1)}, f32[4,64,128]{2,1,0:T(8,128)S(1)}, u32[]{:S(2)}, u32[]{:S(2)}) collective-permute-start(f32[4,64,128]{2,1,0:T(8,128)S(1)} %level5.1.refs_1_), channel_id=1, source_target_pairs={{0,128},{4,132},{8,136},{12,140},{16,144},{20,148},{24,152},{28,15... | collective-permute-start | bytes 393224 | tf_op jit(solution)/shard_map/ppermute | solution.py:274
  38.9 2.4 %collective-permute-start.7 = (f32[4,64,128]{2,1,0:T(8,128)S(1)}, f32[4,64,128]{2,1,0:T(8,128)S(1)}, u32[]{:S(2)}, u32[]{:S(2)}) collective-permute-start(f32[4,64,128]{2,1,0:T(8,128)S(1)} %level5.1.refs_1_), channel_id=1, source_target_pairs={{0,192},{4,196},{8,200},{12,204},{16,208},{20,212},{24,216},{28,22... | collective-permute-start | bytes 393224 | tf_op jit(solution)/shard_map/ppermute | solution.py:274
  41.3 1.3 %collective-permute-done.8 = f32[1,64,512]{2,1,0:T(8,128)S(1)} collective-permute-done((f32[1,64,512]{2,1,0:T(8,128)S(1)}, f32[1,64,512]{2,1,0:T(8,128)S(1)}, u32[]{:S(2)}, u32[]{:S(2)}) %collective-permute-start.8) | collective-permute-done | bytes 131104 | tf_op jit(solution)/shard_map/ppermute | solution.py:314
  42.6 0.2 maximum_multiply_fusion
  42.9 0.8 %fusion = f32[4,128,512]{2,1,0:T(8,128)S(1)} fusion(f32[4,3,256,512]{3,2,1,0:T(8,128)S(1)} %copy-done.2, f32[4,64,256]{2,1,0:T(8,128)S(1)} %get-tuple-element.52, f32[4,64,256]{2,1,0:T(8,128)S(1)} %get-tuple-element.51), kind=kOutput, calls=%fused_computation | convolution fusion | flops 402784256 | bytes 3670016 | tf_op jit(solution)/shard_map/bri,bio->bro/dot_general | solution.py:259
  43.7 0.9 %fusion.12 = f32[4,128,512]{2,1,0:T(8,128)S(1)} fusion(f32[4,128,512]{2,1,0:T(8,128)S(1)} %fusion, f32[4,128,512]{2,1,0:T(8,128)S(1)} %fusion.4.rest_4_, f32[4,3,256,512]{3,2,1,0:T(8,128)S(1)} %copy-done.2, f32[4,64,256]{2,1,0:T(8,128)S(1)} %get-tuple-element.48, f32[4,64,256]{2,1,0:T(8,128)S(1)} %get-tuple-element.47), kind=kOutput, calls=%fused_computation.10 | convolution fusion | flops 403308544 | bytes 5767168 | tf_op jit(solution)/shard_map/bri,bio->bro/dot_general | solution.py:259
  44.7 0.4 part0.1.refs_0_
  45.1 0.4 part1.1.near
  45.4 1.2 %last.1 = f32[4,64,512]{2,1,0:T(8,128)} custom-call(f32[4,64,128]{2,1,0:T(8,128)S(1)} %collective-permute-done.6.two, f32[4,64,128]{2,1,0:T(8,128)S(1)} %collective-permute-done.7.both, bf16[4,4,128,512]{3,2,1,0:T(8,128)(2,1)S(1)} %get-tuple-element.40.rest_0_.refs_2_.high, bf16[4,4,128,512]{3,2,1,0:T(8,128)(2,1)S(1)} %get-tuple-element.41.rest_1_.refs_3_.low, ...), custom_call_target="tpu_custom_call" | custom-call | flops 100000000 | bytes 1000000 | tf_op jit(solution)/shard_map/last/pallas_call | solution.py:243
  (27 shorter events, 0.4 us)
Async XLA Ops:
  0.0 5.6 %copy-start = (f32[8,4,2,64,128]{4,3,2,1,0:T(8,128)S(1)}, f32[8,4,2,64,128]{4,3,2,1,0:T(8,128)}, u32[]{:S(2)}) copy-start(f32[8,4,2,64,128]{4,3,2,1,0:T(8,128)} %weights_ref.3) | copy-start | bytes 6291460
  3.2 3.3 %copy-start.4 = (s32[2,4]{1,0:T(2,128)S(1)}, s32[2,4]{1,0:T(2,128)}, u32[]{:S(2)}) copy-start(s32[2,4]{1,0:T(2,128)} %param.8) | copy-start | bytes 100
  3.2 6.8 %collective-permute-start = (f32[4,64,128]{2,1,0:T(8,128)S(1)}, f32[4,64,128]{2,1,0:T(8,128)S(1)}, u32[]{:S(2)}, u32[]{:S(2)}) collective-permute-start(f32[4,64,128]{2,1,0:T(8,128)S(1)} %get-tuple-element.25.refs_1_.own), channel_id=1, source_target_pairs={{0,4},{4,0},{8,12},{12,8},{16,20},{20,16},{24,28},{28,24},{32,36},... | collective-permute-start | bytes 393224 | tf_op jit(solution)/shard_map/ppermute | solution.py:274
  10.3 5.1 %collective-permute-start.1 = (f32[4,64,128]{2,1,0:T(8,128)S(1)}, f32[4,64,128]{2,1,0:T(8,128)S(1)}, u32[]{:S(2)}, u32[]{:S(2)}) collective-permute-start(f32[4,64,128]{2,1,0:T(8,128)S(1)} %level2.1.refs_1_.own), channel_id=1, source_target_pairs={{0,8},{4,12},{8,0},{12,4},{16,24},{20,28},{24,16},{28,20},{32,40},... | collective-permute-start | bytes 393224 | tf_op jit(solution)/shard_map/ppermute | solution.py:274
  12.3 6.9 %copy-start.3 = (f32[1,4,2,64,128]{4,3,2,1,0:T(8,128)S(1)}, f32[1,4,2,64,128]{4,3,2,1,0:T(8,128)}, u32[]{:S(2)}) copy-start(f32[1,4,2,64,128]{4,3,2,1,0:T(8,128)} %slice.65) | copy-start | bytes 786436
  12.3 10.0 %copy-start.2 = (f32[4,3,256,512]{3,2,1,0:T(8,128)S(1)}, f32[4,3,256,512]{3,2,1,0:T(8,128)}, u32[]{:S(2)}) copy-start(f32[4,3,256,512]{3,2,1,0:T(8,128)} %param.7) | copy-start | bytes 18874372
  12.5 11.4 %collective-permute-start.3 = (f32[1,64,512]{2,1,0:T(8,128)S(1)}, f32[1,64,512]{2,1,0:T(8,128)S(1)}, u32[]{:S(2)}, u32[]{:S(2)}) collective-permute-start(f32[1,64,512]{2,1,0:T(8,128)S(1)} %get-tuple-element.38), channel_id=1, source_target_pairs={{0,4},{4,0},{8,12},{12,8},{16,20},{20,16},{24,28},{28,24},{32,36},... | collective-permute-start | bytes 393224 | tf_op jit(solution)/shard_map/ppermute | solution.py:274
  15.8 8.2 %collective-permute-start.2 = (f32[4,64,128]{2,1,0:T(8,128)S(1)}, f32[4,64,128]{2,1,0:T(8,128)S(1)}, u32[]{:S(2)}, u32[]{:S(2)}) collective-permute-start(f32[4,64,128]{2,1,0:T(8,128)S(1)} %level3.1.refs_1_.own), channel_id=1, source_target_pairs={{0,16},{4,20},{8,24},{12,28},{16,0},{20,4},{24,8},{28,12},{32,48},... | collective-permute-start | bytes 393224 | tf_op jit(solution)/shard_map/ppermute | solution.py:274
  19.2 11.5 %collective-permute-start.5 = (f32[1,4,2,64,128]{4,3,2,1,0:T(8,128)S(1)}, f32[1,4,2,64,128]{4,3,2,1,0:T(8,128)S(1)}, u32[]{:S(2)}, u32[]{:S(2)}) collective-permute-start(f32[1,4,2,64,128]{4,3,2,1,0:T(8,128)S(1)} %copy-done.3), channel_id=1, source_target_pairs={{0,128},{4,132},{8,136},{12,140},{16,144},{20,148},{24,152},{28,15... | collective-permute-start | bytes 786440 | tf_op jit(solution)/shard_map/ppermute | solution.py:274
  22.3 1.0 %copy-start.1 = (f32[4,64,512]{2,1,0:T(8,128)S(1)}, f32[4,64,512]{2,1,0:T(8,128)}, u32[]{:S(2)}) copy-start(f32[4,64,512]{2,1,0:T(8,128)} %expand_ref.1) | copy-start | bytes 1572868
  24.2 12.0 %collective-permute-start.4 = (f32[4,64,128]{2,1,0:T(8,128)S(1)}, f32[4,64,128]{2,1,0:T(8,128)S(1)}, u32[]{:S(2)}, u32[]{:S(2)}) collective-permute-start(f32[4,64,128]{2,1,0:T(8,128)S(1)} %level4.1.after.own), channel_id=1, source_target_pairs={{0,32},{4,36},{8,40},{12,44},{16,48},{20,52},{24,56},{28,60},{32,0... | collective-permute-start | bytes 393224 | tf_op jit(solution)/shard_map/ppermute | solution.py:274
  31.7 10.8 %collective-permute-start.8 = (f32[1,64,512]{2,1,0:T(8,128)S(1)}, f32[1,64,512]{2,1,0:T(8,128)S(1)}, u32[]{:S(2)}, u32[]{:S(2)}) collective-permute-start(f32[1,64,512]{2,1,0:T(8,128)S(1)} %get-tuple-element.42), channel_id=1, source_target_pairs={{0,252},{4,8},{8,4},{12,16},{16,12},{20,24},{24,20},{28,32},{32,28... | collective-permute-start | bytes 393224 | tf_op jit(solution)/shard_map/ppermute | solution.py:314
  36.5 8.6 %collective-permute-start.9 = (f32[4,64,128]{2,1,0:T(8,128)S(1)}, f32[4,64,128]{2,1,0:T(8,128)S(1)}, u32[]{:S(2)}, u32[]{:S(2)}) collective-permute-start(f32[4,64,128]{2,1,0:T(8,128)S(1)} %level5.1.refs_1_), channel_id=1, source_target_pairs={{0,64},{4,68},{8,72},{12,76},{16,80},{20,84},{24,88},{28,92},{32,9... | collective-permute-start | bytes 393224 | tf_op jit(solution)/shard_map/ppermute | solution.py:274
  36.6 8.8 %collective-permute-start.6 = (f32[4,64,128]{2,1,0:T(8,128)S(1)}, f32[4,64,128]{2,1,0:T(8,128)S(1)}, u32[]{:S(2)}, u32[]{:S(2)}) collective-permute-start(f32[4,64,128]{2,1,0:T(8,128)S(1)} %level5.1.refs_1_), channel_id=1, source_target_pairs={{0,128},{4,132},{8,136},{12,140},{16,144},{20,148},{24,152},{28,15... | collective-permute-start | bytes 393224 | tf_op jit(solution)/shard_map/ppermute | solution.py:274
  38.9 6.6 %collective-permute-start.7 = (f32[4,64,128]{2,1,0:T(8,128)S(1)}, f32[4,64,128]{2,1,0:T(8,128)S(1)}, u32[]{:S(2)}, u32[]{:S(2)}) collective-permute-start(f32[4,64,128]{2,1,0:T(8,128)S(1)} %level5.1.refs_1_), channel_id=1, source_target_pairs={{0,192},{4,196},{8,200},{12,204},{16,208},{20,212},{24,216},{28,22... | collective-permute-start | bytes 393224 | tf_op jit(solution)/shard_map/ppermute | solution.py:274

commit v4 on v3

--- a/solution.py
+++ b/solution.py
@@ -311,7 +311,7 @@
 
     other = exchange(coef, 8)
     fused = fuse_two(butterfly, fetched, *last, coef)
-    outer = lax.ppermute(after(jnp.where(even, first, final), fused[0]), "box", pairs)
+    outer = lax.ppermute(after(jnp.where(even, first, final), coef), "box", pairs)
     coef = level_step(coef, other, *level5, "level5", *fused)
 
     two = exchange(coef, 32)

time: 47.5 us -> 46.8 us (0.985)
  no operation moved by 1% of the time
where the time goes in v4:
time: 46.8 us; the launch traced here: 46.3 us
  starting transfers between devices  28.7 us (61%)
  Pallas kernels  8.42 us (18%)
  waiting for transfers between devices  4.97 us (11%)
  matrix products  2.44 us (5%)
  local copies, waits for them, and re-layouts  0.97 us (2%)
    ppermute x9, starting transfers between devices, exchange(): return lax.ppermute(value, 'box', pairs)  24.5 us
    ppermute x1, starting transfers between devices, on_device(): lax.ppermute(after(jnp.where(even, first, final), coef), 'box', pairs)  4.18 us
    ppermute x9, waiting for transfers between devices, exchange(): return lax.ppermute(value, 'box', pairs)  3.86 us
    pallas_call x1, Pallas kernels, head(): pl.pallas_call(head_kernel, out_shape=[pltpu.VMEM((count, rows, width), F...  3.17 us
    dot_general x3, matrix products, product(): jnp.einsum('bri,bio->bro', values, weights, precision=lax.Precision.HIGH)  2.44 us
    pallas_call x1, Pallas kernels, last_step(): pl.pallas_call(last_kernel, out_shape=jax.ShapeDtypeStruct(near.shape, F3...  1.17 us
    ppermute x1, waiting for transfers between devices, on_device(): lax.ppermute(after(jnp.where(even, first, final), coef), 'box', pairs)  1.11 us
    pallas_call x4, Pallas kernels, level_step(): pl.pallas_call(level_kernel, out_shape=pltpu.VMEM(own.shape, F32), in_spe...  1.01 us
  transfers between devices with their start and end apart: 10, of which 3 were waited for; matrix products, arithmetic and copies ran while one was open for 8% of the time, Pallas kernels for 8%

profile of v4, /device:TPU:8, one launch (start us, length us, event | category | flops | bytes accessed | tf_op | source)
XLA Modules:
  0.0 46.3 jit_solution(9216510931588342829)
XLA Ops:
  0.0 3.2 %head.1 = (f32[4,64,128]{2,1,0:T(8,128)S(1)}, f32[4,64,512]{2,1,0:T(8,128)S(1)}) custom-call(f32[4,64,512]{2,1,0:T(8,128)} %x_hbm.1, f32[4,256,128]{2,1,0:T(8,128)} %c_hbm.1, f32[8,4,2,64,128]{4,3,2,1,0:T(8,128)} %weights_ref.3), custom_call_target="tpu_custom_call" | custom-call | flops 250000000 | bytes 2500000 | tf_op jit(solution)/shard_map/head/pallas_call | solution.py:91
  3.2 2.4 %collective-permute-start = (f32[4,64,128]{2,1,0:T(8,128)S(1)}, f32[4,64,128]{2,1,0:T(8,128)S(1)}, u32[]{:S(2)}, u32[]{:S(2)}) collective-permute-start(f32[4,64,128]{2,1,0:T(8,128)S(1)} %get-tuple-element.25.refs_1_.own), channel_id=1, source_target_pairs={{0,4},{4,0},{8,12},{12,8},{16,20},{20,16},{24,28},{28,24},{32,36},... | collective-permute-start | bytes 393224 | tf_op jit(solution)/shard_map/ppermute | solution.py:274
  5.6 0.2 prepare2.1
  5.8 0.7 %slice.65 = f32[1,4,2,64,128]{4,3,2,1,0:T(8,128)} slice(f32[8,4,2,64,128]{4,3,2,1,0:T(8,128)S(1)} %copy-done), slice={[6:7], [0:4], [0:2], [0:64], [0:128]} | slice | bytes 524288 | tf_op jit(solution)/shard_map/slice | solution.py:306
  6.6 3.4 %collective-permute-done.other = f32[4,64,128]{2,1,0:T(8,128)S(1)} collective-permute-done((f32[4,64,128]{2,1,0:T(8,128)S(1)}, f32[4,64,128]{2,1,0:T(8,128)S(1)}, u32[]{:S(2)}, u32[]{:S(2)}) %collective-permute-start) | collective-permute-done | bytes 131104 | tf_op jit(solution)/shard_map/ppermute | solution.py:274
  10.0 0.2 level2.1.refs_1_.own
  10.3 2.0 %collective-permute-start.1 = (f32[4,64,128]{2,1,0:T(8,128)S(1)}, f32[4,64,128]{2,1,0:T(8,128)S(1)}, u32[]{:S(2)}, u32[]{:S(2)}) collective-permute-start(f32[4,64,128]{2,1,0:T(8,128)S(1)} %level2.1.refs_1_.own), channel_id=1, source_target_pairs={{0,8},{4,12},{8,0},{12,4},{16,24},{20,28},{24,16},{28,20},{32,40},... | collective-permute-start | bytes 393224 | tf_op jit(solution)/shard_map/ppermute | solution.py:274
  12.3 0.2 prepare3.1
  12.5 2.4 %collective-permute-start.3 = (f32[1,64,512]{2,1,0:T(8,128)S(1)}, f32[1,64,512]{2,1,0:T(8,128)S(1)}, u32[]{:S(2)}, u32[]{:S(2)}) collective-permute-start(f32[1,64,512]{2,1,0:T(8,128)S(1)} %get-tuple-element.38), channel_id=1, source_target_pairs={{0,4},{4,0},{8,12},{12,8},{16,20},{20,16},{24,28},{28,24},{32,36},... | collective-permute-start | bytes 393224 | tf_op jit(solution)/shard_map/ppermute | solution.py:274
  14.9 0.4 collective-permute-done.1.other
  15.3 0.3 level3.1.refs_1_.own
  15.6 0.2 prepare4.1
  15.8 3.4 %collective-permute-start.2 = (f32[4,64,128]{2,1,0:T(8,128)S(1)}, f32[4,64,128]{2,1,0:T(8,128)S(1)}, u32[]{:S(2)}, u32[]{:S(2)}) collective-permute-start(f32[4,64,128]{2,1,0:T(8,128)S(1)} %level3.1.refs_1_.own), channel_id=1, source_target_pairs={{0,16},{4,20},{8,24},{12,28},{16,0},{20,4},{24,8},{28,12},{32,48},... | collective-permute-start | bytes 393224 | tf_op jit(solution)/shard_map/ppermute | solution.py:274
  19.2 3.1 %collective-permute-start.5 = (f32[1,4,2,64,128]{4,3,2,1,0:T(8,128)S(1)}, f32[1,4,2,64,128]{4,3,2,1,0:T(8,128)S(1)}, u32[]{:S(2)}, u32[]{:S(2)}) collective-permute-start(f32[1,4,2,64,128]{4,3,2,1,0:T(8,128)S(1)} %copy-done.3), channel_id=1, source_target_pairs={{0,128},{4,132},{8,136},{12,140},{16,144},{20,148},{24,152},{28,15... | collective-permute-start | bytes 786440 | tf_op jit(solution)/shard_map/ppermute | solution.py:274
  22.3 0.8 %fusion.4.rest_4_ = f32[4,128,512]{2,1,0:T(8,128)S(1)} fusion(f32[4,3,256,512]{3,2,1,0:T(8,128)S(1)} %copy-done.2, f32[4,64,256]{2,1,0:T(8,128)S(1)} %get-tuple-element.56, f32[4,64,256]{2,1,0:T(8,128)S(1)} %get-tuple-element.55), kind=kOutput, calls=%fused_computation.4 | convolution fusion | flops 402784256 | bytes 3670016 | tf_op jit(solution)/shard_map/bri,bio->bro/dot_general | solution.py:259
  23.1 0.2 prepare5.1
  23.4 0.6 %fuse_last.1 = (bf16[4,2,128,512]{3,2,1,0:T(8,128)(2,1)S(1)}, bf16[4,2,128,512]{3,2,1,0:T(8,128)(2,1)S(1)}) custom-call(f32[8,4,2,64,128]{4,3,2,1,0:T(8,128)S(1)} %copy-done, f32[4,64,512]{2,1,0:T(8,128)S(1)} %copy-done.1, bf16[4,256,128]{2,1,0:T(8,128)(2,1)S(1)} %get-tuple-element.30.after.high), custom_call_target="tpu_custom_call" | custom-call | flops 100000000 | bytes 1000000 | tf_op jit(solution)/shard_map/fuse_last/pallas_call | solution.py:154
  24.0 0.3 level4.1.after.own
  24.2 6.5 %collective-permute-start.4 = (f32[4,64,128]{2,1,0:T(8,128)S(1)}, f32[4,64,128]{2,1,0:T(8,128)S(1)}, u32[]{:S(2)}, u32[]{:S(2)}) collective-permute-start(f32[4,64,128]{2,1,0:T(8,128)S(1)} %level4.1.after.own), channel_id=1, source_target_pairs={{0,32},{4,36},{8,40},{12,44},{16,48},{20,52},{24,56},{28,60},{32,0... | collective-permute-start | bytes 393224 | tf_op jit(solution)/shard_map/ppermute | solution.py:274
  30.7 4.2 %collective-permute-start.8 = (f32[1,64,512]{2,1,0:T(8,128)S(1)}, f32[1,64,512]{2,1,0:T(8,128)S(1)}, u32[]{:S(2)}, u32[]{:S(2)}) collective-permute-start(f32[1,64,512]{2,1,0:T(8,128)S(1)} %get-tuple-element.42), channel_id=1, source_target_pairs={{0,252},{4,8},{8,4},{12,16},{16,12},{20,24},{24,20},{28,32},{32,28... | collective-permute-start | bytes 393224 | tf_op jit(solution)/shard_map/ppermute | solution.py:314
  34.9 1.0 %fuse_two.1 = (bf16[4,4,128,512]{3,2,1,0:T(8,128)(2,1)S(1)}, bf16[4,4,128,512]{3,2,1,0:T(8,128)(2,1)S(1)}) custom-call(f32[8,4,2,64,128]{4,3,2,1,0:T(8,128)S(1)} %copy-done, f32[1,4,2,64,128]{4,3,2,1,0:T(8,128)S(1)} %collective-permute-done.5.fetched_ref, bf16[4,2,128,512]{3,2,1,0:T(8,128)(2,1)S(1)} %get-tuple-element.34.rest_2_.m_high, ...), custom_call_target="tpu_custom_call" | custom-call | flops 150000000 | bytes 1500000 | tf_op jit(solution)/shard_map/fuse_two/pallas_call | solution.py:180
  35.9 0.3 level5.1.refs_1_
  36.2 0.1 collective-permute-start.9
  36.3 2.3 %collective-permute-start.6 = (f32[4,64,128]{2,1,0:T(8,128)S(1)}, f32[4,64,128]{2,1,0:T(8,128)S(1)}, u32[]{:S(2)}, u32[]{:S(2)}) collective-permute-start(f32[4,64,128]{2,1,0:T(8,128)S(1)} %level5.1.refs_1_), channel_id=1, source_target_pairs={{0,128},{4,132},{8,136},{12,140},{16,144},{20,148},{24,152},{28,15... | collective-permute-start | bytes 393224 | tf_op jit(solution)/shard_map/ppermute | solution.py:274
  38.6 2.4 %collective-permute-start.7 = (f32[4,64,128]{2,1,0:T(8,128)S(1)}, f32[4,64,128]{2,1,0:T(8,128)S(1)}, u32[]{:S(2)}, u32[]{:S(2)}) collective-permute-start(f32[4,64,128]{2,1,0:T(8,128)S(1)} %level5.1.refs_1_), channel_id=1, source_target_pairs={{0,192},{4,196},{8,200},{12,204},{16,208},{20,212},{24,216},{28,22... | collective-permute-start | bytes 393224 | tf_op jit(solution)/shard_map/ppermute | solution.py:274
  41.0 1.1 %collective-permute-done.8 = f32[1,64,512]{2,1,0:T(8,128)S(1)} collective-permute-done((f32[1,64,512]{2,1,0:T(8,128)S(1)}, f32[1,64,512]{2,1,0:T(8,128)S(1)}, u32[]{:S(2)}, u32[]{:S(2)}) %collective-permute-start.8) | collective-permute-done | bytes 131104 | tf_op jit(solution)/shard_map/ppermute | solution.py:314
  42.1 0.2 maximum_multiply_fusion
  42.4 0.8 %fusion = f32[4,128,512]{2,1,0:T(8,128)S(1)} fusion(f32[4,3,256,512]{3,2,1,0:T(8,128)S(1)} %copy-done.2, f32[4,64,256]{2,1,0:T(8,128)S(1)} %get-tuple-element.52, f32[4,64,256]{2,1,0:T(8,128)S(1)} %get-tuple-element.51), kind=kOutput, calls=%fused_computation | convolution fusion | flops 402784256 | bytes 3670016 | tf_op jit(solution)/shard_map/bri,bio->bro/dot_general | solution.py:259
  43.2 0.9 %fusion.12 = f32[4,128,512]{2,1,0:T(8,128)S(1)} fusion(f32[4,128,512]{2,1,0:T(8,128)S(1)} %fusion, f32[4,128,512]{2,1,0:T(8,128)S(1)} %fusion.4.rest_4_, f32[4,3,256,512]{3,2,1,0:T(8,128)S(1)} %copy-done.2, f32[4,64,256]{2,1,0:T(8,128)S(1)} %get-tuple-element.48, f32[4,64,256]{2,1,0:T(8,128)S(1)} %get-tuple-element.47), kind=kOutput, calls=%fused_computation.10 | convolution fusion | flops 403308544 | bytes 5767168 | tf_op jit(solution)/shard_map/bri,bio->bro/dot_general | solution.py:259
  44.2 0.4 part0.1.refs_0_
  44.6 0.4 part1.1.near
  44.9 1.2 %last.1 = f32[4,64,512]{2,1,0:T(8,128)} custom-call(f32[4,64,128]{2,1,0:T(8,128)S(1)} %collective-permute-done.6.two, f32[4,64,128]{2,1,0:T(8,128)S(1)} %collective-permute-done.7.both, bf16[4,4,128,512]{3,2,1,0:T(8,128)(2,1)S(1)} %get-tuple-element.40.rest_0_.refs_2_.high, bf16[4,4,128,512]{3,2,1,0:T(8,128)(2,1)S(1)} %get-tuple-element.41.rest_1_.refs_3_.low, ...), custom_call_target="tpu_custom_call" | custom-call | flops 100000000 | bytes 1000000 | tf_op jit(solution)/shard_map/last/pallas_call | solution.py:243
  (27 shorter events, 0.4 us)
Async XLA Ops:
  0.0 5.6 %copy-start = (f32[8,4,2,64,128]{4,3,2,1,0:T(8,128)S(1)}, f32[8,4,2,64,128]{4,3,2,1,0:T(8,128)}, u32[]{:S(2)}) copy-start(f32[8,4,2,64,128]{4,3,2,1,0:T(8,128)} %weights_ref.3) | copy-start | bytes 6291460
  3.2 3.3 %copy-start.4 = (s32[2,4]{1,0:T(2,128)S(1)}, s32[2,4]{1,0:T(2,128)}, u32[]{:S(2)}) copy-start(s32[2,4]{1,0:T(2,128)} %param.8) | copy-start | bytes 100
  3.2 6.8 %collective-permute-start = (f32[4,64,128]{2,1,0:T(8,128)S(1)}, f32[4,64,128]{2,1,0:T(8,128)S(1)}, u32[]{:S(2)}, u32[]{:S(2)}) collective-permute-start(f32[4,64,128]{2,1,0:T(8,128)S(1)} %get-tuple-element.25.refs_1_.own), channel_id=1, source_target_pairs={{0,4},{4,0},{8,12},{12,8},{16,20},{20,16},{24,28},{28,24},{32,36},... | collective-permute-start | bytes 393224 | tf_op jit(solution)/shard_map/ppermute | solution.py:274
  10.3 5.1 %collective-permute-start.1 = (f32[4,64,128]{2,1,0:T(8,128)S(1)}, f32[4,64,128]{2,1,0:T(8,128)S(1)}, u32[]{:S(2)}, u32[]{:S(2)}) collective-permute-start(f32[4,64,128]{2,1,0:T(8,128)S(1)} %level2.1.refs_1_.own), channel_id=1, source_target_pairs={{0,8},{4,12},{8,0},{12,4},{16,24},{20,28},{24,16},{28,20},{32,40},... | collective-permute-start | bytes 393224 | tf_op jit(solution)/shard_map/ppermute | solution.py:274
  12.3 6.9 %copy-start.3 = (f32[1,4,2,64,128]{4,3,2,1,0:T(8,128)S(1)}, f32[1,4,2,64,128]{4,3,2,1,0:T(8,128)}, u32[]{:S(2)}) copy-start(f32[1,4,2,64,128]{4,3,2,1,0:T(8,128)} %slice.65) | copy-start | bytes 786436
  12.3 10.0 %copy-start.2 = (f32[4,3,256,512]{3,2,1,0:T(8,128)S(1)}, f32[4,3,256,512]{3,2,1,0:T(8,128)}, u32[]{:S(2)}) copy-start(f32[4,3,256,512]{3,2,1,0:T(8,128)} %param.7) | copy-start | bytes 18874372
  12.5 11.4 %collective-permute-start.3 = (f32[1,64,512]{2,1,0:T(8,128)S(1)}, f32[1,64,512]{2,1,0:T(8,128)S(1)}, u32[]{:S(2)}, u32[]{:S(2)}) collective-permute-start(f32[1,64,512]{2,1,0:T(8,128)S(1)} %get-tuple-element.38), channel_id=1, source_target_pairs={{0,4},{4,0},{8,12},{12,8},{16,20},{20,16},{24,28},{28,24},{32,36},... | collective-permute-start | bytes 393224 | tf_op jit(solution)/shard_map/ppermute | solution.py:274
  15.8 8.2 %collective-permute-start.2 = (f32[4,64,128]{2,1,0:T(8,128)S(1)}, f32[4,64,128]{2,1,0:T(8,128)S(1)}, u32[]{:S(2)}, u32[]{:S(2)}) collective-permute-start(f32[4,64,128]{2,1,0:T(8,128)S(1)} %level3.1.refs_1_.own), channel_id=1, source_target_pairs={{0,16},{4,20},{8,24},{12,28},{16,0},{20,4},{24,8},{28,12},{32,48},... | collective-permute-start | bytes 393224 | tf_op jit(solution)/shard_map/ppermute | solution.py:274
  19.2 15.7 %collective-permute-start.5 = (f32[1,4,2,64,128]{4,3,2,1,0:T(8,128)S(1)}, f32[1,4,2,64,128]{4,3,2,1,0:T(8,128)S(1)}, u32[]{:S(2)}, u32[]{:S(2)}) collective-permute-start(f32[1,4,2,64,128]{4,3,2,1,0:T(8,128)S(1)} %copy-done.3), channel_id=1, source_target_pairs={{0,128},{4,132},{8,136},{12,140},{16,144},{20,148},{24,152},{28,15... | collective-permute-start | bytes 786440 | tf_op jit(solution)/shard_map/ppermute | solution.py:274
  22.3 1.0 %copy-start.1 = (f32[4,64,512]{2,1,0:T(8,128)S(1)}, f32[4,64,512]{2,1,0:T(8,128)}, u32[]{:S(2)}) copy-start(f32[4,64,512]{2,1,0:T(8,128)} %expand_ref.1) | copy-start | bytes 1572868
  24.2 11.7 %collective-permute-start.4 = (f32[4,64,128]{2,1,0:T(8,128)S(1)}, f32[4,64,128]{2,1,0:T(8,128)S(1)}, u32[]{:S(2)}, u32[]{:S(2)}) collective-permute-start(f32[4,64,128]{2,1,0:T(8,128)S(1)} %level4.1.after.own), channel_id=1, source_target_pairs={{0,32},{4,36},{8,40},{12,44},{16,48},{20,52},{24,56},{28,60},{32,0... | collective-permute-start | bytes 393224 | tf_op jit(solution)/shard_map/ppermute | solution.py:274
  30.7 11.3 %collective-permute-start.8 = (f32[1,64,512]{2,1,0:T(8,128)S(1)}, f32[1,64,512]{2,1,0:T(8,128)S(1)}, u32[]{:S(2)}, u32[]{:S(2)}) collective-permute-start(f32[1,64,512]{2,1,0:T(8,128)S(1)} %get-tuple-element.42), channel_id=1, source_target_pairs={{0,252},{4,8},{8,4},{12,16},{16,12},{20,24},{24,20},{28,32},{32,28... | collective-permute-start | bytes 393224 | tf_op jit(solution)/shard_map/ppermute | solution.py:314
  36.2 8.4 %collective-permute-start.9 = (f32[4,64,128]{2,1,0:T(8,128)S(1)}, f32[4,64,128]{2,1,0:T(8,128)S(1)}, u32[]{:S(2)}, u32[]{:S(2)}) collective-permute-start(f32[4,64,128]{2,1,0:T(8,128)S(1)} %level5.1.refs_1_), channel_id=1, source_target_pairs={{0,64},{4,68},{8,72},{12,76},{16,80},{20,84},{24,88},{28,92},{32,9... | collective-permute-start | bytes 393224 | tf_op jit(solution)/shard_map/ppermute | solution.py:274
  36.3 8.6 %collective-permute-start.6 = (f32[4,64,128]{2,1,0:T(8,128)S(1)}, f32[4,64,128]{2,1,0:T(8,128)S(1)}, u32[]{:S(2)}, u32[]{:S(2)}) collective-permute-start(f32[4,64,128]{2,1,0:T(8,128)S(1)} %level5.1.refs_1_), channel_id=1, source_target_pairs={{0,128},{4,132},{8,136},{12,140},{16,144},{20,148},{24,152},{28,15... | collective-permute-start | bytes 393224 | tf_op jit(solution)/shard_map/ppermute | solution.py:274
  38.6 6.4 %collective-permute-start.7 = (f32[4,64,128]{2,1,0:T(8,128)S(1)}, f32[4,64,128]{2,1,0:T(8,128)S(1)}, u32[]{:S(2)}, u32[]{:S(2)}) collective-permute-start(f32[4,64,128]{2,1,0:T(8,128)S(1)} %level5.1.refs_1_), channel_id=1, source_target_pairs={{0,192},{4,196},{8,200},{12,204},{16,208},{20,212},{24,216},{28,22... | collective-permute-start | bytes 393224 | tf_op jit(solution)/shard_map/ppermute | solution.py:274

commit v5 on v4

--- a/solution.py
+++ b/solution.py
@@ -37,8 +37,13 @@
 def apply_split(values, high, low):
     rows = values.shape[0]
     first, second = split(values)
-    both = dot(jnp.concatenate([first, second], axis=0), high)
-    return both[:rows] + (both[rows:] + dot(first, low))
+    left = jnp.concatenate([first, second], axis=0)
+    width = high.shape[1]
+    if width > 128:
+        both = dot(left, high)
+        return both[:rows] + (both[rows:] + dot(first, low))
+    both = dot(left, jnp.concatenate([high, low], axis=1))
+    return both[:rows, :width] + (both[rows:, :width] + both[:rows, width:])
 
 
 def complex_dot(values, weights):
@@ -303,7 +308,7 @@
 
     other = exchange(coef, 4)
     level4 = weights(4, coef)
-    fetched = exchange(after(butterfly[6:7], level4[0]), 32)
+    fetched = exchange(after(butterfly[6:7], coef), 32)
     near = product(stacked(after(x, level4[0])), near_blocks[:, 1])
     level5 = weights(5, coef)
     last = fuse_last(butterfly, expand, level4[0])

time: 46.8 us -> 46.8 us (level)
  no operation moved by 1% of the time
where the time goes in v5:
time: 46.8 us; the launch traced here: 46.3 us
  starting transfers between devices  28.7 us (61%)
  Pallas kernels  8.42 us (18%)
  waiting for transfers between devices  4.96 us (11%)
  matrix products  2.44 us (5%)
  local copies, waits for them, and re-layouts  0.97 us (2%)
    ppermute x9, starting transfers between devices, exchange(): return lax.ppermute(value, 'box', pairs)  24.5 us
    ppermute x1, starting transfers between devices, on_device(): lax.ppermute(after(jnp.where(even, first, final), coef), 'box', pairs)  4.19 us
    ppermute x9, waiting for transfers between devices, exchange(): return lax.ppermute(value, 'box', pairs)  3.86 us
    pallas_call x1, Pallas kernels, head(): pl.pallas_call(head_kernel, out_shape=[pltpu.VMEM((count, rows, width), F...  3.24 us
    dot_general x3, matrix products, product(): jnp.einsum('bri,bio->bro', values, weights, precision=lax.Precision.HIGH)  2.44 us
    pallas_call x1, Pallas kernels, last_step(): pl.pallas_call(last_kernel, out_shape=jax.ShapeDtypeStruct(near.shape, F3...  1.18 us
    ppermute x1, waiting for transfers between devices, on_device(): lax.ppermute(after(jnp.where(even, first, final), coef), 'box', pairs)  1.1 us
    pallas_call x1, Pallas kernels, fuse_two(): pl.pallas_call(fuse_two_kernel, out_shape=[shape, shape], in_specs=[VMEM]...  0.99 us
  transfers between devices with their start and end apart: 10, of which 3 were waited for; matrix products, arithmetic and copies ran while one was open for 8% of the time, Pallas kernels for 8%

profile of v5, /device:TPU:8, one launch (start us, length us, event | category | flops | bytes accessed | tf_op | source)
XLA Modules:
  0.0 46.3 jit_solution(17712126294056195608)
XLA Ops:
  0.0 3.2 %head.1 = (f32[4,64,128]{2,1,0:T(8,128)S(1)}, f32[4,64,512]{2,1,0:T(8,128)S(1)}) custom-call(f32[4,64,512]{2,1,0:T(8,128)} %x_hbm.1, f32[4,256,128]{2,1,0:T(8,128)} %c_hbm.1, f32[8,4,2,64,128]{4,3,2,1,0:T(8,128)} %weights_ref.3), custom_call_target="tpu_custom_call" | custom-call | flops 250000000 | bytes 2500000 | tf_op jit(solution)/shard_map/head/pallas_call | solution.py:96
  3.3 2.4 %collective-permute-start = (f32[4,64,128]{2,1,0:T(8,128)S(1)}, f32[4,64,128]{2,1,0:T(8,128)S(1)}, u32[]{:S(2)}, u32[]{:S(2)}) collective-permute-start(f32[4,64,128]{2,1,0:T(8,128)S(1)} %get-tuple-element.25.refs_1_.own), channel_id=1, source_target_pairs={{0,4},{4,0},{8,12},{12,8},{16,20},{20,16},{24,28},{28,24},{32,36},... | collective-permute-start | bytes 393224 | tf_op jit(solution)/shard_map/ppermute | solution.py:279
  5.6 0.2 prepare2.1
  5.9 0.7 %slice.65 = f32[1,4,2,64,128]{4,3,2,1,0:T(8,128)} slice(f32[8,4,2,64,128]{4,3,2,1,0:T(8,128)S(1)} %copy-done), slice={[6:7], [0:4], [0:2], [0:64], [0:128]} | slice | bytes 524288 | tf_op jit(solution)/shard_map/slice | solution.py:311
  6.7 3.4 %collective-permute-done.other = f32[4,64,128]{2,1,0:T(8,128)S(1)} collective-permute-done((f32[4,64,128]{2,1,0:T(8,128)S(1)}, f32[4,64,128]{2,1,0:T(8,128)S(1)}, u32[]{:S(2)}, u32[]{:S(2)}) %collective-permute-start) | collective-permute-done | bytes 131104 | tf_op jit(solution)/shard_map/ppermute | solution.py:279
  10.1 0.2 level2.1.refs_1_.own
  10.3 2.0 %collective-permute-start.1 = (f32[4,64,128]{2,1,0:T(8,128)S(1)}, f32[4,64,128]{2,1,0:T(8,128)S(1)}, u32[]{:S(2)}, u32[]{:S(2)}) collective-permute-start(f32[4,64,128]{2,1,0:T(8,128)S(1)} %level2.1.refs_1_.own), channel_id=1, source_target_pairs={{0,8},{4,12},{8,0},{12,4},{16,24},{20,28},{24,16},{28,20},{32,40},... | collective-permute-start | bytes 393224 | tf_op jit(solution)/shard_map/ppermute | solution.py:279
  12.4 0.2 prepare3.1
  12.6 2.4 %collective-permute-start.3 = (f32[1,64,512]{2,1,0:T(8,128)S(1)}, f32[1,64,512]{2,1,0:T(8,128)S(1)}, u32[]{:S(2)}, u32[]{:S(2)}) collective-permute-start(f32[1,64,512]{2,1,0:T(8,128)S(1)} %get-tuple-element.38), channel_id=1, source_target_pairs={{0,4},{4,0},{8,12},{12,8},{16,20},{20,16},{24,28},{28,24},{32,36},... | collective-permute-start | bytes 393224 | tf_op jit(solution)/shard_map/ppermute | solution.py:279
  15.0 0.4 collective-permute-done.1.other
  15.4 0.2 level3.1.refs_1_.own
  15.6 0.2 prepare4.1
  15.8 3.4 %collective-permute-start.2 = (f32[4,64,128]{2,1,0:T(8,128)S(1)}, f32[4,64,128]{2,1,0:T(8,128)S(1)}, u32[]{:S(2)}, u32[]{:S(2)}) collective-permute-start(f32[4,64,128]{2,1,0:T(8,128)S(1)} %level3.1.refs_1_.own), channel_id=1, source_target_pairs={{0,16},{4,20},{8,24},{12,28},{16,0},{20,4},{24,8},{28,12},{32,48},... | collective-permute-start | bytes 393224 | tf_op jit(solution)/shard_map/ppermute | solution.py:279
  19.3 3.1 %collective-permute-start.5 = (f32[1,4,2,64,128]{4,3,2,1,0:T(8,128)S(1)}, f32[1,4,2,64,128]{4,3,2,1,0:T(8,128)S(1)}, u32[]{:S(2)}, u32[]{:S(2)}) collective-permute-start(f32[1,4,2,64,128]{4,3,2,1,0:T(8,128)S(1)} %copy-done.3), channel_id=1, source_target_pairs={{0,128},{4,132},{8,136},{12,140},{16,144},{20,148},{24,152},{28,15... | collective-permute-start | bytes 786440 | tf_op jit(solution)/shard_map/ppermute | solution.py:279
  22.4 0.8 %fusion.4.rest_4_ = f32[4,128,512]{2,1,0:T(8,128)S(1)} fusion(f32[4,3,256,512]{3,2,1,0:T(8,128)S(1)} %copy-done.2, f32[4,64,256]{2,1,0:T(8,128)S(1)} %get-tuple-element.56, f32[4,64,256]{2,1,0:T(8,128)S(1)} %get-tuple-element.55), kind=kOutput, calls=%fused_computation.4 | convolution fusion | flops 402784256 | bytes 3670016 | tf_op jit(solution)/shard_map/bri,bio->bro/dot_general | solution.py:264
  23.2 0.2 prepare5.1
  23.4 0.6 %fuse_last.1 = (bf16[4,2,128,512]{3,2,1,0:T(8,128)(2,1)S(1)}, bf16[4,2,128,512]{3,2,1,0:T(8,128)(2,1)S(1)}) custom-call(f32[8,4,2,64,128]{4,3,2,1,0:T(8,128)S(1)} %copy-done, f32[4,64,512]{2,1,0:T(8,128)S(1)} %copy-done.1, bf16[4,256,128]{2,1,0:T(8,128)(2,1)S(1)} %get-tuple-element.30.after.high), custom_call_target="tpu_custom_call" | custom-call | flops 100000000 | bytes 1000000 | tf_op jit(solution)/shard_map/fuse_last/pallas_call | solution.py:159
  24.0 0.2 level4.1.after.own
  24.3 6.5 %collective-permute-start.4 = (f32[4,64,128]{2,1,0:T(8,128)S(1)}, f32[4,64,128]{2,1,0:T(8,128)S(1)}, u32[]{:S(2)}, u32[]{:S(2)}) collective-permute-start(f32[4,64,128]{2,1,0:T(8,128)S(1)} %level4.1.after.own), channel_id=1, source_target_pairs={{0,32},{4,36},{8,40},{12,44},{16,48},{20,52},{24,56},{28,60},{32,0... | collective-permute-start | bytes 393224 | tf_op jit(solution)/shard_map/ppermute | solution.py:279
  30.7 4.2 %collective-permute-start.8 = (f32[1,64,512]{2,1,0:T(8,128)S(1)}, f32[1,64,512]{2,1,0:T(8,128)S(1)}, u32[]{:S(2)}, u32[]{:S(2)}) collective-permute-start(f32[1,64,512]{2,1,0:T(8,128)S(1)} %get-tuple-element.42), channel_id=1, source_target_pairs={{0,252},{4,8},{8,4},{12,16},{16,12},{20,24},{24,20},{28,32},{32,28... | collective-permute-start | bytes 393224 | tf_op jit(solution)/shard_map/ppermute | solution.py:319
  34.9 1.0 %fuse_two.1 = (bf16[4,4,128,512]{3,2,1,0:T(8,128)(2,1)S(1)}, bf16[4,4,128,512]{3,2,1,0:T(8,128)(2,1)S(1)}) custom-call(f32[8,4,2,64,128]{4,3,2,1,0:T(8,128)S(1)} %copy-done, f32[1,4,2,64,128]{4,3,2,1,0:T(8,128)S(1)} %collective-permute-done.5.fetched_ref, bf16[4,2,128,512]{3,2,1,0:T(8,128)(2,1)S(1)} %get-tuple-element.34.rest_2_.m_high, ...), custom_call_target="tpu_custom_call" | custom-call | flops 150000000 | bytes 1500000 | tf_op jit(solution)/shard_map/fuse_two/pallas_call | solution.py:185
  36.0 0.2 level5.1.refs_1_
  36.2 0.1 collective-permute-start.9
  36.3 2.3 %collective-permute-start.6 = (f32[4,64,128]{2,1,0:T(8,128)S(1)}, f32[4,64,128]{2,1,0:T(8,128)S(1)}, u32[]{:S(2)}, u32[]{:S(2)}) collective-permute-start(f32[4,64,128]{2,1,0:T(8,128)S(1)} %level5.1.refs_1_), channel_id=1, source_target_pairs={{0,128},{4,132},{8,136},{12,140},{16,144},{20,148},{24,152},{28,15... | collective-permute-start | bytes 393224 | tf_op jit(solution)/shard_map/ppermute | solution.py:279
  38.6 2.4 %collective-permute-start.7 = (f32[4,64,128]{2,1,0:T(8,128)S(1)}, f32[4,64,128]{2,1,0:T(8,128)S(1)}, u32[]{:S(2)}, u32[]{:S(2)}) collective-permute-start(f32[4,64,128]{2,1,0:T(8,128)S(1)} %level5.1.refs_1_), channel_id=1, source_target_pairs={{0,192},{4,196},{8,200},{12,204},{16,208},{20,212},{24,216},{28,22... | collective-permute-start | bytes 393224 | tf_op jit(solution)/shard_map/ppermute | solution.py:279
  41.0 1.1 %collective-permute-done.8 = f32[1,64,512]{2,1,0:T(8,128)S(1)} collective-permute-done((f32[1,64,512]{2,1,0:T(8,128)S(1)}, f32[1,64,512]{2,1,0:T(8,128)S(1)}, u32[]{:S(2)}, u32[]{:S(2)}) %collective-permute-start.8) | collective-permute-done | bytes 131104 | tf_op jit(solution)/shard_map/ppermute | solution.py:319
  42.1 0.2 maximum_multiply_fusion
  42.4 0.8 %fusion = f32[4,128,512]{2,1,0:T(8,128)S(1)} fusion(f32[4,3,256,512]{3,2,1,0:T(8,128)S(1)} %copy-done.2, f32[4,64,256]{2,1,0:T(8,128)S(1)} %get-tuple-element.52, f32[4,64,256]{2,1,0:T(8,128)S(1)} %get-tuple-element.51), kind=kOutput, calls=%fused_computation | convolution fusion | flops 402784256 | bytes 3670016 | tf_op jit(solution)/shard_map/bri,bio->bro/dot_general | solution.py:264
  43.2 0.9 %fusion.12 = f32[4,128,512]{2,1,0:T(8,128)S(1)} fusion(f32[4,128,512]{2,1,0:T(8,128)S(1)} %fusion, f32[4,128,512]{2,1,0:T(8,128)S(1)} %fusion.4.rest_4_, f32[4,3,256,512]{3,2,1,0:T(8,128)S(1)} %copy-done.2, f32[4,64,256]{2,1,0:T(8,128)S(1)} %get-tuple-element.48, f32[4,64,256]{2,1,0:T(8,128)S(1)} %get-tuple-element.47), kind=kOutput, calls=%fused_computation.10 | convolution fusion | flops 403308544 | bytes 5767168 | tf_op jit(solution)/shard_map/bri,bio->bro/dot_general | solution.py:264
  44.2 0.4 part0.1.refs_0_
  44.6 0.4 part1.1.near
  45.0 1.2 %last.1 = f32[4,64,512]{2,1,0:T(8,128)} custom-call(f32[4,64,128]{2,1,0:T(8,128)S(1)} %collective-permute-done.6.two, f32[4,64,128]{2,1,0:T(8,128)S(1)} %collective-permute-done.7.both, bf16[4,4,128,512]{3,2,1,0:T(8,128)(2,1)S(1)} %get-tuple-element.40.rest_0_.refs_2_.high, bf16[4,4,128,512]{3,2,1,0:T(8,128)(2,1)S(1)} %get-tuple-element.41.rest_1_.refs_3_.low, ...), custom_call_target="tpu_custom_call" | custom-call | flops 100000000 | bytes 1000000 | tf_op jit(solution)/shard_map/last/pallas_call | solution.py:248
  (27 shorter events, 0.4 us)
Async XLA Ops:
  0.0 5.6 %copy-start = (f32[8,4,2,64,128]{4,3,2,1,0:T(8,128)S(1)}, f32[8,4,2,64,128]{4,3,2,1,0:T(8,128)}, u32[]{:S(2)}) copy-start(f32[8,4,2,64,128]{4,3,2,1,0:T(8,128)} %weights_ref.3) | copy-start | bytes 6291460
  3.2 3.3 %copy-start.4 = (s32[2,4]{1,0:T(2,128)S(1)}, s32[2,4]{1,0:T(2,128)}, u32[]{:S(2)}) copy-start(s32[2,4]{1,0:T(2,128)} %param.8) | copy-start | bytes 100
  3.3 6.8 %collective-permute-start = (f32[4,64,128]{2,1,0:T(8,128)S(1)}, f32[4,64,128]{2,1,0:T(8,128)S(1)}, u32[]{:S(2)}, u32[]{:S(2)}) collective-permute-start(f32[4,64,128]{2,1,0:T(8,128)S(1)} %get-tuple-element.25.refs_1_.own), channel_id=1, source_target_pairs={{0,4},{4,0},{8,12},{12,8},{16,20},{20,16},{24,28},{28,24},{32,36},... | collective-permute-start | bytes 393224 | tf_op jit(solution)/shard_map/ppermute | solution.py:279
  10.3 5.1 %collective-permute-start.1 = (f32[4,64,128]{2,1,0:T(8,128)S(1)}, f32[4,64,128]{2,1,0:T(8,128)S(1)}, u32[]{:S(2)}, u32[]{:S(2)}) collective-permute-start(f32[4,64,128]{2,1,0:T(8,128)S(1)} %level2.1.refs_1_.own), channel_id=1, source_target_pairs={{0,8},{4,12},{8,0},{12,4},{16,24},{20,28},{24,16},{28,20},{32,40},... | collective-permute-start | bytes 393224 | tf_op jit(solution)/shard_map/ppermute | solution.py:279
  12.3 6.9 %copy-start.3 = (f32[1,4,2,64,128]{4,3,2,1,0:T(8,128)S(1)}, f32[1,4,2,64,128]{4,3,2,1,0:T(8,128)}, u32[]{:S(2)}) copy-start(f32[1,4,2,64,128]{4,3,2,1,0:T(8,128)} %slice.65) | copy-start | bytes 786436
  12.4 10.0 %copy-start.2 = (f32[4,3,256,512]{3,2,1,0:T(8,128)S(1)}, f32[4,3,256,512]{3,2,1,0:T(8,128)}, u32[]{:S(2)}) copy-start(f32[4,3,256,512]{3,2,1,0:T(8,128)} %param.7) | copy-start | bytes 18874372
  12.6 11.4 %collective-permute-start.3 = (f32[1,64,512]{2,1,0:T(8,128)S(1)}, f32[1,64,512]{2,1,0:T(8,128)S(1)}, u32[]{:S(2)}, u32[]{:S(2)}) collective-permute-start(f32[1,64,512]{2,1,0:T(8,128)S(1)} %get-tuple-element.38), channel_id=1, source_target_pairs={{0,4},{4,0},{8,12},{12,8},{16,20},{20,16},{24,28},{28,24},{32,36},... | collective-permute-start | bytes 393224 | tf_op jit(solution)/shard_map/ppermute | solution.py:279
  15.8 8.2 %collective-permute-start.2 = (f32[4,64,128]{2,1,0:T(8,128)S(1)}, f32[4,64,128]{2,1,0:T(8,128)S(1)}, u32[]{:S(2)}, u32[]{:S(2)}) collective-permute-start(f32[4,64,128]{2,1,0:T(8,128)S(1)} %level3.1.refs_1_.own), channel_id=1, source_target_pairs={{0,16},{4,20},{8,24},{12,28},{16,0},{20,4},{24,8},{28,12},{32,48},... | collective-permute-start | bytes 393224 | tf_op jit(solution)/shard_map/ppermute | solution.py:279
  19.3 15.7 %collective-permute-start.5 = (f32[1,4,2,64,128]{4,3,2,1,0:T(8,128)S(1)}, f32[1,4,2,64,128]{4,3,2,1,0:T(8,128)S(1)}, u32[]{:S(2)}, u32[]{:S(2)}) collective-permute-start(f32[1,4,2,64,128]{4,3,2,1,0:T(8,128)S(1)} %copy-done.3), channel_id=1, source_target_pairs={{0,128},{4,132},{8,136},{12,140},{16,144},{20,148},{24,152},{28,15... | collective-permute-start | bytes 786440 | tf_op jit(solution)/shard_map/ppermute | solution.py:279
  22.4 1.0 %copy-start.1 = (f32[4,64,512]{2,1,0:T(8,128)S(1)}, f32[4,64,512]{2,1,0:T(8,128)}, u32[]{:S(2)}) copy-start(f32[4,64,512]{2,1,0:T(8,128)} %expand_ref.1) | copy-start | bytes 1572868
  24.3 11.7 %collective-permute-start.4 = (f32[4,64,128]{2,1,0:T(8,128)S(1)}, f32[4,64,128]{2,1,0:T(8,128)S(1)}, u32[]{:S(2)}, u32[]{:S(2)}) collective-permute-start(f32[4,64,128]{2,1,0:T(8,128)S(1)} %level4.1.after.own), channel_id=1, source_target_pairs={{0,32},{4,36},{8,40},{12,44},{16,48},{20,52},{24,56},{28,60},{32,0... | collective-permute-start | bytes 393224 | tf_op jit(solution)/shard_map/ppermute | solution.py:279
  30.7 11.3 %collective-permute-start.8 = (f32[1,64,512]{2,1,0:T(8,128)S(1)}, f32[1,64,512]{2,1,0:T(8,128)S(1)}, u32[]{:S(2)}, u32[]{:S(2)}) collective-permute-start(f32[1,64,512]{2,1,0:T(8,128)S(1)} %get-tuple-element.42), channel_id=1, source_target_pairs={{0,252},{4,8},{8,4},{12,16},{16,12},{20,24},{24,20},{28,32},{32,28... | collective-permute-start | bytes 393224 | tf_op jit(solution)/shard_map/ppermute | solution.py:319
  36.2 8.4 %collective-permute-start.9 = (f32[4,64,128]{2,1,0:T(8,128)S(1)}, f32[4,64,128]{2,1,0:T(8,128)S(1)}, u32[]{:S(2)}, u32[]{:S(2)}) collective-permute-start(f32[4,64,128]{2,1,0:T(8,128)S(1)} %level5.1.refs_1_), channel_id=1, source_target_pairs={{0,64},{4,68},{8,72},{12,76},{16,80},{20,84},{24,88},{28,92},{32,9... | collective-permute-start | bytes 393224 | tf_op jit(solution)/shard_map/ppermute | solution.py:279
  36.3 8.6 %collective-permute-start.6 = (f32[4,64,128]{2,1,0:T(8,128)S(1)}, f32[4,64,128]{2,1,0:T(8,128)S(1)}, u32[]{:S(2)}, u32[]{:S(2)}) collective-permute-start(f32[4,64,128]{2,1,0:T(8,128)S(1)} %level5.1.refs_1_), channel_id=1, source_target_pairs={{0,128},{4,132},{8,136},{12,140},{16,144},{20,148},{24,152},{28,15... | collective-permute-start | bytes 393224 | tf_op jit(solution)/shard_map/ppermute | solution.py:279
  38.6 6.4 %collective-permute-start.7 = (f32[4,64,128]{2,1,0:T(8,128)S(1)}, f32[4,64,128]{2,1,0:T(8,128)S(1)}, u32[]{:S(2)}, u32[]{:S(2)}) collective-permute-start(f32[4,64,128]{2,1,0:T(8,128)S(1)} %level5.1.refs_1_), channel_id=1, source_target_pairs={{0,192},{4,196},{8,200},{12,204},{16,208},{20,212},{24,216},{28,22... | collective-permute-start | bytes 393224 | tf_op jit(solution)/shard_map/ppermute | solution.py:279
